TPU v7x, 128 devices: a whole 4x4x4 slice. The times are simulated.
128 devices in a mesh: tiles: 128 (over x, z, y, core).
Axes of the slice: x: 4, y: 4, z: 4, core: 2. Of those that a mesh axis runs over, the one named last changes fastest.
Arguments:
- water_depth: float32 [512, 128, 128], P('tiles'), may hold values from 0.05 to 2
- velocity: float32 [512, 2, 128, 128], P('tiles'), may hold values from -22 to 22
- aquifer_head: float32 [512, 128, 128], P('tiles'), may hold values from -3 to -0.5
- terrain: float32 [512, 128, 128], P('tiles'), may hold values from -1.5 to 1.5
- leakance: float32 [512, 128, 128], P('tiles'), may hold values from 0.05 to 0.5
- diffusivity: float32 [512, 128, 128], P('tiles'), may hold values from 0.1 to 1
- tile_wet: int32 [512], replicated, may hold values from 0 to 1, as said below
- neighbours: int32 [512, 4], replicated, may hold values from -1 to 511, as said below
- destination: int32 [512], replicated, may hold values from 0 to 511, as said below
Outputs:
- flood_depth: float32 [512, 128, 128], P('tiles')
- flood_discharge: float32 [512, 2, 128, 128], P('tiles')
- water_table: float32 [512, 128, 128], P('tiles')
Inputs may be any that keep to these rules, and one draw needn't show every extreme that they name: `tile_wet`: 1 marks a tile that holds water. `neighbours`: slot t lies in row t // 16 of the basin's tile layout, at column t % 16 in even rows and 15 - t % 16 in odd rows. Entry k (west, east, south, north) names the slot of the tile beside it in that direction, or -1 where there is none or where either of the two tiles is dry. The relation is mutual. `destination`: A permutation. Slot s belongs to device s // 4. Tiles move only between neighbouring devices, by swaps: between devices k and k + 1 the same number of tiles pass each way, at most 2, exactly 2 between devices 0 and 1.
All inputs are finite; a program needn't handle non-finite values.
Results may differ from a plain program's by a relative error of at most 0.00002.
Values sent between devices are 32-bit elements; how exact they have to be, the bound alone decides.
A program may use at most 128 MiB of HBM per device.

v0:
```python
import math

import jax
import jax.numpy as jnp
from jax import lax
from jax.sharding import PartitionSpec as P

TPD = 4
MOVE = 2
STEPS = 4
SPAN = 10


GRAVITY = 9.81
SHALLOW = 0.1
COURANT = 0.45
STORAGE = 0.2
WALL_SIGNS = (
    (1.0, -1.0, 1.0, 1.0, 1.0),
    (1.0, -1.0, 1.0, 1.0, 1.0),
    (1.0, 1.0, -1.0, 1.0, 1.0),
    (1.0, 1.0, -1.0, 1.0, 1.0),
)
FACING = (1, 0, 3, 2)


def passed_along(value, axis, steps):
    count = lax.axis_size(axis)
    initial, last = (max(0, -steps), min(count, count - steps))
    return lax.ppermute(value, axis, [(source, source + steps) for source in range(initial, last)])


def face_flux(depth_left, normal_left, along_left, depth_right, normal_right, along_right):
    floor_left = jnp.maximum(depth_left, SHALLOW)
    floor_right = jnp.maximum(depth_right, SHALLOW)
    speed_left = normal_left / floor_left
    speed_right = normal_right / floor_right
    wave_speed = jnp.maximum(
        jnp.abs(speed_left) + jnp.sqrt(GRAVITY * floor_left),
        jnp.abs(speed_right) + jnp.sqrt(GRAVITY * floor_right),
    )
    mass_flux = 0.5 * (normal_left + normal_right) - 0.5 * wave_speed * (depth_right - depth_left)
    push_flux = 0.5 * (
        normal_left * speed_left
        + 0.5 * GRAVITY * depth_left * depth_left
        + normal_right * speed_right
        + 0.5 * GRAVITY * depth_right * depth_right
    ) - 0.5 * wave_speed * (normal_right - normal_left)
    carry_flux = 0.5 * (along_left * speed_left + along_right * speed_right) - 0.5 * wave_speed * (
        along_right - along_left
    )
    return (mass_flux, push_flux, carry_flux)


def east_side(field, ghost):
    return jnp.concatenate([field[:, 1:], ghost[:, None]], axis=1)


def west_side(field, ghost):
    return jnp.concatenate([ghost[:, None], field[:, :-1]], axis=1)


def north_side(field, ghost):
    return jnp.concatenate([field[1:], ghost[None]], axis=0)


def south_side(field, ghost):
    return jnp.concatenate([ghost[None], field[:-1]], axis=0)


def advance(fields_now, ground, leak_rate, spread, ghosts, interval):
    water_now = fields_now[0]
    east_flow = fields_now[1]
    north_flow = fields_now[2]
    head_now = fields_now[3]
    cells = (water_now, east_flow, north_flow, head_now, ground)
    east_cells = [east_side(cells[field_index], ghosts[1, field_index]) for field_index in range(5)]
    north_cells = [
        north_side(cells[field_index], ghosts[3, field_index]) for field_index in range(5)
    ]
    west_head = west_side(head_now, ghosts[0, 3])
    west_ground = west_side(ground, ghosts[0, 4])
    south_head = south_side(head_now, ghosts[2, 3])
    south_ground = south_side(ground, ghosts[2, 4])
    flux_east = face_flux(
        water_now, east_flow, north_flow, east_cells[0], east_cells[1], east_cells[2]
    )
    rim_west = face_flux(
        ghosts[0, 0], ghosts[0, 1], ghosts[0, 2], water_now[:, 0], east_flow[:, 0], north_flow[:, 0]
    )
    flux_west = [
        jnp.concatenate([rim_west[part_index][:, None], flux_east[part_index][:, :-1]], axis=1)
        for part_index in range(3)
    ]
    flux_north = face_flux(
        water_now, north_flow, east_flow, north_cells[0], north_cells[2], north_cells[1]
    )
    rim_south = face_flux(
        ghosts[2, 0], ghosts[2, 2], ghosts[2, 1], water_now[0], north_flow[0], east_flow[0]
    )
    flux_south = [
        jnp.concatenate([rim_south[part_index][None], flux_north[part_index][:-1]], axis=0)
        for part_index in range(3)
    ]
    seepage = leak_rate * (water_now + ground - head_now)
    new_depth = (
        water_now
        - interval * (flux_east[0] - flux_west[0] + (flux_north[0] - flux_south[0]))
        - interval * seepage
    )
    new_east = (
        east_flow
        - interval * (flux_east[1] - flux_west[1] + (flux_north[2] - flux_south[2]))
        - interval * GRAVITY * water_now * 0.5 * (east_cells[4] - west_ground)
    )
    new_north = (
        north_flow
        - interval * (flux_east[2] - flux_west[2] + (flux_north[1] - flux_south[1]))
        - interval * GRAVITY * water_now * 0.5 * (north_cells[4] - south_ground)
    )
    new_head = head_now + interval * (
        spread * (east_cells[3] + west_head + north_cells[3] + south_head - 4.0 * head_now)
        + seepage / STORAGE
    )
    return jnp.stack([new_depth, new_east, new_north, new_head])


def tile_speed(fields_now):
    floor_depth = jnp.maximum(fields_now[..., 0, :, :], SHALLOW)
    cell_speed = (
        jnp.abs(fields_now[..., 1, :, :]) / floor_depth
        + jnp.abs(fields_now[..., 2, :, :]) / floor_depth
        + 2.0 * jnp.sqrt(GRAVITY * floor_depth)
    )
    return jnp.max(cell_speed, axis=(-2, -1))


def tile_edges(fields_now):
    return jnp.stack(
        [
            fields_now[..., :, 0],
            fields_now[..., :, -1],
            fields_now[..., 0, :],
            fields_now[..., -1, :],
        ],
        axis=-3,
    )


def pick_rims(received, source_rank, within):
    facing = jnp.array(FACING, jnp.int32)[None, :]
    flattened = received.reshape((-1,) + received.shape[3:])
    lookup = (
        jnp.clip(source_rank, 0, received.shape[0] - 1) * received.shape[1] + within
    ) * 4 + facing
    return jnp.take(flattened, lookup.reshape(-1), axis=0).reshape(
        within.shape + received.shape[3:]
    )


def shards(
    water_depth,
    velocity,
    aquifer_head,
    terrain,
    leakance,
    diffusivity,
    tile_wet,
    neighbours,
    destination,
):
    device = lax.axis_index("tiles")
    slots_total = destination.shape[0]
    all_slots = jnp.arange(slots_total, dtype=jnp.int32)
    owner_before = all_slots // TPD
    owner_after = destination // TPD
    source = jnp.zeros((slots_total,), jnp.int32).at[destination].set(all_slots)
    discharge = water_depth[:, None] * velocity
    packed = jnp.concatenate(
        [
            water_depth[:, None],
            discharge,
            aquifer_head[:, None],
            terrain[:, None],
            leakance[:, None],
            diffusivity[:, None],
        ],
        axis=1,
    )
    rightward = (owner_after > owner_before).astype(jnp.int32).reshape(-1, TPD)
    leftward = (owner_after < owner_before).astype(jnp.int32).reshape(-1, TPD)
    rank_right = (jnp.cumsum(rightward, axis=1) - rightward).reshape(-1)
    rank_left = (jnp.cumsum(leftward, axis=1) - leftward).reshape(-1)
    base_slot = device * TPD
    positions = jnp.arange(MOVE, dtype=jnp.int32)[:, None]
    local_slots = jnp.arange(TPD, dtype=jnp.int32)

    def outgoing(flags, ranks):
        mine_flags = lax.dynamic_slice_in_dim(flags.reshape(-1), base_slot, TPD)
        mine_ranks = lax.dynamic_slice_in_dim(ranks, base_slot, TPD)
        matches = mine_flags[None, :] * (mine_ranks[None, :] == positions).astype(jnp.int32)
        chosen = jnp.sum(matches * local_slots[None, :], axis=1)
        return jnp.take(packed, chosen, axis=0)

    from_left = passed_along(outgoing(rightward, rank_right), "tiles", 1)
    from_right = passed_along(outgoing(leftward, rank_left), "tiles", -1)
    pool_tiles = jnp.concatenate([packed, from_left, from_right], axis=0)
    arrived_tiles = lax.dynamic_slice_in_dim(source, base_slot, TPD)
    came_owner = arrived_tiles // TPD
    pick_slot = jnp.where(
        came_owner == device,
        arrived_tiles % TPD,
        jnp.where(
            came_owner < device,
            TPD + rank_right[arrived_tiles],
            TPD + MOVE + rank_left[arrived_tiles],
        ),
    )
    migrated = jnp.take(pool_tiles, pick_slot, axis=0)
    fields_now = migrated[:, :4]
    ground = migrated[:, 4]
    leak_rate = migrated[:, 5]
    spread = migrated[:, 6]
    wet_slot = tile_wet[arrived_tiles]
    linked = neighbours[arrived_tiles]
    linked_slots = jnp.where(linked >= 0, destination[jnp.clip(linked, 0, slots_total - 1)], -1)
    owners = linked_slots // TPD
    within = linked_slots % TPD
    wall_signs = jnp.array(WALL_SIGNS, jnp.float32)[:, :, None]
    lowest = 2.0 * math.sqrt(GRAVITY * SHALLOW)
    ground_rims = tile_edges(ground[:, None])
    stepper = jax.vmap(advance, in_axes=(0, 0, 0, 0, 0, None))
    for index_step in range(STEPS):
        fastest = lax.pmax(
            jnp.max(jnp.where(wet_slot == 1, tile_speed(fields_now), lowest)), "tiles"
        )
        interval = COURANT / fastest
        field_rims = tile_edges(fields_now)
        rim_rows = jnp.concatenate([field_rims, ground_rims], axis=2)
        blocks = []
        for offset in range(-SPAN, SPAN + 1):
            if offset == 0:
                blocks.append(rim_rows[None])
            else:
                blocks.append(passed_along(rim_rows, "tiles", -offset)[None])
        received = jnp.concatenate(blocks, axis=0)
        remote_rims = pick_rims(received, owners - device + SPAN, within)
        ghosts = jnp.where(
            (linked_slots >= 0)[:, :, None, None], remote_rims, rim_rows * wall_signs
        )
        updated = stepper(fields_now, ground, leak_rate, spread, ghosts, interval)
        fields_now = jnp.where((wet_slot == 1)[:, None, None, None], updated, fields_now)
    return (fields_now[:, 0], fields_now[:, 1:3], fields_now[:, 3])


def solution(mesh):
    placed = (
        P("tiles", None, None),
        P("tiles", None, None, None),
        P("tiles", None, None),
        P("tiles", None, None),
        P("tiles", None, None),
        P("tiles", None, None),
        P(),
        P(),
        P(),
    )
    return jax.shard_map(
        shards,
        mesh=mesh,
        in_specs=placed,
        out_specs=(P("tiles", None, None), P("tiles", None, None, None), P("tiles", None, None)),
        check_vma=False,
    )
```

profile of v0, /device:TPU:0, one launch (start us, length us, event | category | flops | bytes accessed | tf_op | source)
XLA Modules:
  0.0 970.7 jit_solution(9509762514406306317)
XLA Ops:
  9.9 3.2 collective-permute-start
  20.2 3.5 pad_maximum_fusion
  23.6 3.9 gather_fusion.3
  36.0 10.9 %collective-permute-start.2 = (f32[4,4,5,128]{3,0,2,1:T(4,128)S(1)}, f32[4,4,5,128]{3,0,2,1:T(4,128)}, u32[]{:S(2)}, u32[]{:S(2)}) collective-permute-start(f32[4,4,5,128]{3,0,2,1:T(4,128)S(1)} %maximum_maximum_fusion.3), channel_id=1, source_target_pairs={{0,10},{1,11},{2,12},{3,13},{4,14},{5,15},{6,16},{7,17},{8,18},{9,... | collective-permute-start | bytes 122888 | tf_op jit(solution)/shard_map/ppermute | solution.py:30
  46.9 3.1 collective-permute-start.3
  50.0 3.8 collective-permute-start.4
  53.8 8.0 collective-permute-start.5
  61.8 7.7 collective-permute-start.6
  89.0 3.7 collective-permute-start.8
  98.9 3.5 collective-permute-start.11
  113.9 3.3 collective-permute-done.15
  123.0 3.4 collective-permute-done.19
  127.8 3.7 collective-permute-done.21
  147.9 3.9 maximum_multiply_fusion.18
  159.3 77.3 %pmax.28 = f32[]{:T(128)} all-reduce(f32[]{:T(128)} %select_reduce_fusion.3), channel_id=1, replica_groups=mesh['tiles'=128] {'tiles'}, use_global_device_ids=true, to_apply=%region_7.9 | all-reduce | flops 1 | bytes 8 | tf_op jit(solution)/shard_map/pmax | solution.py:234
  246.7 3.5 fusion.38
  275.0 6.4 collective-permute-start.25
  281.4 3.9 collective-permute-start.26
  293.8 5.4 collective-permute-start.28
  300.6 3.7 collective-permute-start.30
  328.7 3.8 collective-permute-done.39
  360.4 3.8 maximum_multiply_fusion.10
  365.6 76.0 %pmax.29 = f32[]{:T(128)} all-reduce(f32[]{:T(128)} %select_reduce_fusion.2), channel_id=1, replica_groups=mesh['tiles'=128] {'tiles'}, use_global_device_ids=true, to_apply=%region_10.13 | all-reduce | flops 1 | bytes 8 | tf_op jit(solution)/shard_map/pmax | solution.py:234
  471.5 4.0 collective-permute-start.43
  478.5 5.6 collective-permute-start.45
  484.1 3.4 collective-permute-start.46
  493.1 63.2 %pmax.30 = f32[]{:T(128)} all-reduce(f32[]{:T(128)} %select_reduce_fusion.1), channel_id=1, replica_groups=mesh['tiles'=128] {'tiles'}, use_global_device_ids=true, to_apply=%region_13.16 | all-reduce | flops 1 | bytes 8 | tf_op jit(solution)/shard_map/pmax | solution.py:234
  570.1 3.8 collective-permute-start.48
  576.8 4.3 collective-permute-start.50
  596.6 3.3 collective-permute-done.55
  605.7 3.4 collective-permute-done.59
  610.6 3.1 collective-permute-done.61
  638.1 3.5 fusion.328
  676.8 4.2 fusion.70
  686.7 4.0 fusion.158
  708.2 6.4 collective-permute-start.62
  714.6 4.4 collective-permute-start.63
  719.1 5.4 collective-permute-start.64
  724.5 7.5 collective-permute-start.65
  732.0 4.3 collective-permute-start.66
  762.2 3.3 collective-permute-start.68
  769.5 6.9 collective-permute-start.70
  792.8 3.3 collective-permute-done.75
  802.0 3.4 collective-permute-done.79
  806.9 3.1 collective-permute-done.81
  834.4 3.3 fusion.117
  848.1 74.8 %pmax.31 = f32[]{:T(128)} all-reduce(f32[]{:T(128)} %select_reduce_fusion), channel_id=1, replica_groups=mesh['tiles'=128] {'tiles'}, use_global_device_ids=true, to_apply=%region_16.19 | all-reduce | flops 1 | bytes 8 | tf_op jit(solution)/shard_map/pmax | solution.py:234
  939.7 3.1 multiply_subtract_fusion.1
  (952 shorter events, 479.2 us)
Async XLA Ops:
  6.9 13.3 %collective-permute-start.1 = (f32[2,7,128,128]{3,2,1,0:T(8,128)}, f32[2,7,128,128]{3,2,1,0:T(8,128)}, u32[]{:S(2)}, u32[]{:S(2)}) collective-permute-start(f32[2,7,128,128]{3,2,1,0:T(8,128)} %broadcast_select_fusion), channel_id=1, source_target_pairs={{1,0},{2,1},{3,2},{4,3},{5,4},{6,5},{7,6},{8,7},{9,8},{10,9},{11,1... | collective-permute-start | bytes 2752520 | tf_op jit(solution)/shard_map/ppermute | solution.py:30
  36.0 50.9 %collective-permute-start.2 = (f32[4,4,5,128]{3,0,2,1:T(4,128)S(1)}, f32[4,4,5,128]{3,0,2,1:T(4,128)}, u32[]{:S(2)}, u32[]{:S(2)}) collective-permute-start(f32[4,4,5,128]{3,0,2,1:T(4,128)S(1)} %maximum_maximum_fusion.3), channel_id=1, source_target_pairs={{0,10},{1,11},{2,12},{3,13},{4,14},{5,15},{6,16},{7,17},{8,18},{9,... | collective-permute-start | bytes 122888 | tf_op jit(solution)/shard_map/ppermute | solution.py:30
  46.9 42.1 %collective-permute-start.3 = (f32[4,4,5,128]{3,0,2,1:T(4,128)S(1)}, f32[4,4,5,128]{3,0,2,1:T(4,128)}, u32[]{:S(2)}, u32[]{:S(2)}) collective-permute-start(f32[4,4,5,128]{3,0,2,1:T(4,128)S(1)} %maximum_maximum_fusion.3), channel_id=1, source_target_pairs={{0,9},{1,10},{2,11},{3,12},{4,13},{5,14},{6,15},{7,16},{8,17},{9,1... | collective-permute-start | bytes 122888 | tf_op jit(solution)/shard_map/ppermute | solution.py:30
  50.0 43.5 %collective-permute-start.4 = (f32[4,4,5,128]{3,0,2,1:T(4,128)S(1)}, f32[4,4,5,128]{3,0,2,1:T(4,128)}, u32[]{:S(2)}, u32[]{:S(2)}) collective-permute-start(f32[4,4,5,128]{3,0,2,1:T(4,128)S(1)} %maximum_maximum_fusion.3), channel_id=1, source_target_pairs={{0,8},{1,9},{2,10},{3,11},{4,12},{5,13},{6,14},{7,15},{8,16},{9,17... | collective-permute-start | bytes 122888 | tf_op jit(solution)/shard_map/ppermute | solution.py:30
  53.8 41.8 %collective-permute-start.5 = (f32[4,4,5,128]{3,0,2,1:T(4,128)S(1)}, f32[4,4,5,128]{3,0,2,1:T(4,128)}, u32[]{:S(2)}, u32[]{:S(2)}) collective-permute-start(f32[4,4,5,128]{3,0,2,1:T(4,128)S(1)} %maximum_maximum_fusion.3), channel_id=1, source_target_pairs={{0,7},{1,8},{2,9},{3,10},{4,11},{5,12},{6,13},{7,14},{8,15},{9,16}... | collective-permute-start | bytes 122888 | tf_op jit(solution)/shard_map/ppermute | solution.py:30
  61.8 37.2 %collective-permute-start.6 = (f32[4,4,5,128]{3,0,2,1:T(4,128)S(1)}, f32[4,4,5,128]{3,0,2,1:T(4,128)S(1)}, u32[]{:S(2)}, u32[]{:S(2)}) collective-permute-start(f32[4,4,5,128]{3,0,2,1:T(4,128)S(1)} %maximum_maximum_fusion.3), channel_id=1, source_target_pairs={{0,6},{1,7},{2,8},{3,9},{4,10},{5,11},{6,12},{7,13},{8,14},{9,15},... | collective-permute-start | bytes 122888 | tf_op jit(solution)/shard_map/ppermute | solution.py:30
  86.9 15.6 %collective-permute-start.7 = (f32[4,4,5,128]{3,0,2,1:T(4,128)S(1)}, f32[4,4,5,128]{3,0,2,1:T(4,128)S(1)}, u32[]{:S(2)}, u32[]{:S(2)}) collective-permute-start(f32[4,4,5,128]{3,0,2,1:T(4,128)S(1)} %maximum_maximum_fusion.3), channel_id=1, source_target_pairs={{0,5},{1,6},{2,7},{3,8},{4,9},{5,10},{6,11},{7,12},{8,13},{9,14},{... | collective-permute-start | bytes 122888 | tf_op jit(solution)/shard_map/ppermute | solution.py:30
  89.0 14.8 %collective-permute-start.8 = (f32[4,4,5,128]{3,0,2,1:T(4,128)S(1)}, f32[4,4,5,128]{3,0,2,1:T(4,128)S(1)}, u32[]{:S(2)}, u32[]{:S(2)}) collective-permute-start(f32[4,4,5,128]{3,0,2,1:T(4,128)S(1)} %maximum_maximum_fusion.3), channel_id=1, source_target_pairs={{0,4},{1,5},{2,6},{3,7},{4,8},{5,9},{6,10},{7,11},{8,12},{9,13},{1... | collective-permute-start | bytes 122888 | tf_op jit(solution)/shard_map/ppermute | solution.py:30
  109.2 12.3 %collective-permute-start.17 = (f32[4,4,5,128]{3,0,2,1:T(4,128)S(1)}, f32[4,4,5,128]{3,0,2,1:T(4,128)S(1)}, u32[]{:S(2)}, u32[]{:S(2)}) collective-permute-start(f32[4,4,5,128]{3,0,2,1:T(4,128)S(1)} %maximum_maximum_fusion.3), channel_id=1, source_target_pairs={{6,0},{7,1},{8,2},{9,3},{10,4},{11,5},{12,6},{13,7},{14,8},{15,9},... | collective-permute-start | bytes 122888 | tf_op jit(solution)/shard_map/ppermute | solution.py:30
  111.2 11.8 %collective-permute-start.18 = (f32[4,4,5,128]{3,0,2,1:T(4,128)S(1)}, f32[4,4,5,128]{3,0,2,1:T(4,128)S(1)}, u32[]{:S(2)}, u32[]{:S(2)}) collective-permute-start(f32[4,4,5,128]{3,0,2,1:T(4,128)S(1)} %maximum_maximum_fusion.3), channel_id=1, source_target_pairs={{7,0},{8,1},{9,2},{10,3},{11,4},{12,5},{13,6},{14,7},{15,8},{16,9}... | collective-permute-start | bytes 122888 | tf_op jit(solution)/shard_map/ppermute | solution.py:30
  112.6 13.9 %collective-permute-start.19 = (f32[4,4,5,128]{3,0,2,1:T(4,128)S(1)}, f32[4,4,5,128]{3,0,2,1:T(4,128)S(1)}, u32[]{:S(2)}, u32[]{:S(2)}) collective-permute-start(f32[4,4,5,128]{3,0,2,1:T(4,128)S(1)} %maximum_maximum_fusion.3), channel_id=1, source_target_pairs={{8,0},{9,1},{10,2},{11,3},{12,4},{13,5},{14,6},{15,7},{16,8},{17,9... | collective-permute-start | bytes 122888 | tf_op jit(solution)/shard_map/ppermute | solution.py:30
  118.5 13.0 %collective-permute-start.21 = (f32[4,4,5,128]{3,0,2,1:T(4,128)S(1)}, f32[4,4,5,128]{3,0,2,1:T(4,128)S(1)}, u32[]{:S(2)}, u32[]{:S(2)}) collective-permute-start(f32[4,4,5,128]{3,0,2,1:T(4,128)S(1)} %maximum_maximum_fusion.3), channel_id=1, source_target_pairs={{10,0},{11,1},{12,2},{13,3},{14,4},{15,5},{16,6},{17,7},{18,8},{19... | collective-permute-start | bytes 122888 | tf_op jit(solution)/shard_map/ppermute | solution.py:30
  267.1 25.1 %collective-permute-start.22 = (f32[4,4,5,128]{3,0,2,1:T(4,128)S(1)}, f32[4,4,5,128]{3,0,2,1:T(4,128)S(1)}, u32[]{:S(2)}, u32[]{:S(2)}) collective-permute-start(f32[4,4,5,128]{3,0,2,1:T(4,128)S(1)} %maximum_maximum_fusion.4), channel_id=1, source_target_pairs={{0,10},{1,11},{2,12},{3,13},{4,14},{5,15},{6,16},{7,17},{8,18},{9,... | collective-permute-start | bytes 122888 | tf_op jit(solution)/shard_map/ppermute | solution.py:30
  270.1 23.7 %collective-permute-start.23 = (f32[4,4,5,128]{3,0,2,1:T(4,128)S(1)}, f32[4,4,5,128]{3,0,2,1:T(4,128)S(1)}, u32[]{:S(2)}, u32[]{:S(2)}) collective-permute-start(f32[4,4,5,128]{3,0,2,1:T(4,128)S(1)} %maximum_maximum_fusion.4), channel_id=1, source_target_pairs={{0,9},{1,10},{2,11},{3,12},{4,13},{5,14},{6,15},{7,16},{8,17},{9,1... | collective-permute-start | bytes 122888 | tf_op jit(solution)/shard_map/ppermute | solution.py:30
  272.2 27.1 %collective-permute-start.24 = (f32[4,4,5,128]{3,0,2,1:T(4,128)S(1)}, f32[4,4,5,128]{3,0,2,1:T(4,128)S(1)}, u32[]{:S(2)}, u32[]{:S(2)}) collective-permute-start(f32[4,4,5,128]{3,0,2,1:T(4,128)S(1)} %maximum_maximum_fusion.4), channel_id=1, source_target_pairs={{0,8},{1,9},{2,10},{3,11},{4,12},{5,13},{6,14},{7,15},{8,16},{9,17... | collective-permute-start | bytes 122888 | tf_op jit(solution)/shard_map/ppermute | solution.py:30
  275.0 25.7 %collective-permute-start.25 = (f32[4,4,5,128]{3,0,2,1:T(4,128)S(1)}, f32[4,4,5,128]{3,0,2,1:T(4,128)S(1)}, u32[]{:S(2)}, u32[]{:S(2)}) collective-permute-start(f32[4,4,5,128]{3,0,2,1:T(4,128)S(1)} %maximum_maximum_fusion.4), channel_id=1, source_target_pairs={{0,7},{1,8},{2,9},{3,10},{4,11},{5,12},{6,13},{7,14},{8,15},{9,16}... | collective-permute-start | bytes 122888 | tf_op jit(solution)/shard_map/ppermute | solution.py:30
  281.4 23.0 %collective-permute-start.26 = (f32[4,4,5,128]{3,0,2,1:T(4,128)S(1)}, f32[4,4,5,128]{3,0,2,1:T(4,128)S(1)}, u32[]{:S(2)}, u32[]{:S(2)}) collective-permute-start(f32[4,4,5,128]{3,0,2,1:T(4,128)S(1)} %maximum_maximum_fusion.4), channel_id=1, source_target_pairs={{0,6},{1,7},{2,8},{3,9},{4,10},{5,11},{6,12},{7,13},{8,14},{9,15},... | collective-permute-start | bytes 122888 | tf_op jit(solution)/shard_map/ppermute | solution.py:30
  292.3 15.0 %collective-permute-start.27 = (f32[4,4,5,128]{3,0,2,1:T(4,128)S(1)}, f32[4,4,5,128]{3,0,2,1:T(4,128)S(1)}, u32[]{:S(2)}, u32[]{:S(2)}) collective-permute-start(f32[4,4,5,128]{3,0,2,1:T(4,128)S(1)} %maximum_maximum_fusion.4), channel_id=1, source_target_pairs={{0,5},{1,6},{2,7},{3,8},{4,9},{5,10},{6,11},{7,12},{8,13},{9,14},{... | collective-permute-start | bytes 122888 | tf_op jit(solution)/shard_map/ppermute | solution.py:30
  293.8 14.8 %collective-permute-start.28 = (f32[4,4,5,128]{3,0,2,1:T(4,128)S(1)}, f32[4,4,5,128]{3,0,2,1:T(4,128)S(1)}, u32[]{:S(2)}, u32[]{:S(2)}) collective-permute-start(f32[4,4,5,128]{3,0,2,1:T(4,128)S(1)} %maximum_maximum_fusion.4), channel_id=1, source_target_pairs={{0,4},{1,5},{2,6},{3,7},{4,8},{5,9},{6,10},{7,11},{8,12},{9,13},{1... | collective-permute-start | bytes 122888 | tf_op jit(solution)/shard_map/ppermute | solution.py:30
  313.9 13.4 %collective-permute-start.37 = (f32[4,4,5,128]{3,0,2,1:T(4,128)S(1)}, f32[4,4,5,128]{3,0,2,1:T(4,128)S(1)}, u32[]{:S(2)}, u32[]{:S(2)}) collective-permute-start(f32[4,4,5,128]{3,0,2,1:T(4,128)S(1)} %maximum_maximum_fusion.4), channel_id=1, source_target_pairs={{6,0},{7,1},{8,2},{9,3},{10,4},{11,5},{12,6},{13,7},{14,8},{15,9},... | collective-permute-start | bytes 122888 | tf_op jit(solution)/shard_map/ppermute | solution.py:30
  318.4 14.0 %collective-permute-start.39 = (f32[4,4,5,128]{3,0,2,1:T(4,128)S(1)}, f32[4,4,5,128]{3,0,2,1:T(4,128)S(1)}, u32[]{:S(2)}, u32[]{:S(2)}) collective-permute-start(f32[4,4,5,128]{3,0,2,1:T(4,128)S(1)} %maximum_maximum_fusion.4), channel_id=1, source_target_pairs={{8,0},{9,1},{10,2},{11,3},{12,4},{13,5},{14,6},{15,7},{16,8},{17,9... | collective-permute-start | bytes 122888 | tf_op jit(solution)/shard_map/ppermute | solution.py:30
  324.1 12.7 %collective-permute-start.41 = (f32[4,4,5,128]{3,0,2,1:T(4,128)S(1)}, f32[4,4,5,128]{3,0,2,1:T(4,128)S(1)}, u32[]{:S(2)}, u32[]{:S(2)}) collective-permute-start(f32[4,4,5,128]{3,0,2,1:T(4,128)S(1)} %maximum_maximum_fusion.4), channel_id=1, source_target_pairs={{10,0},{11,1},{12,2},{13,3},{14,4},{15,5},{16,6},{17,7},{18,8},{19... | collective-permute-start | bytes 122888 | tf_op jit(solution)/shard_map/ppermute | solution.py:30
  468.9 97.8 %collective-permute-start.42 = (f32[4,4,5,128]{3,0,2,1:T(4,128)S(1)}, f32[4,4,5,128]{3,0,2,1:T(4,128)}, u32[]{:S(2)}, u32[]{:S(2)}) collective-permute-start(f32[4,4,5,128]{3,0,2,1:T(4,128)S(1)} %maximum_maximum_fusion.5), channel_id=1, source_target_pairs={{0,10},{1,11},{2,12},{3,13},{4,14},{5,15},{6,16},{7,17},{8,18},{9,... | collective-permute-start | bytes 122888 | tf_op jit(solution)/shard_map/ppermute | solution.py:30
  471.5 98.6 %collective-permute-start.43 = (f32[4,4,5,128]{3,0,2,1:T(4,128)S(1)}, f32[4,4,5,128]{3,0,2,1:T(4,128)}, u32[]{:S(2)}, u32[]{:S(2)}) collective-permute-start(f32[4,4,5,128]{3,0,2,1:T(4,128)S(1)} %maximum_maximum_fusion.5), channel_id=1, source_target_pairs={{0,9},{1,10},{2,11},{3,12},{4,13},{5,14},{6,15},{7,16},{8,17},{9,1... | collective-permute-start | bytes 122888 | tf_op jit(solution)/shard_map/ppermute | solution.py:30
  475.5 99.2 %collective-permute-start.44 = (f32[4,4,5,128]{3,0,2,1:T(4,128)S(1)}, f32[4,4,5,128]{3,0,2,1:T(4,128)}, u32[]{:S(2)}, u32[]{:S(2)}) collective-permute-start(f32[4,4,5,128]{3,0,2,1:T(4,128)S(1)} %maximum_maximum_fusion.5), channel_id=1, source_target_pairs={{0,8},{1,9},{2,10},{3,11},{4,12},{5,13},{6,14},{7,15},{8,16},{9,17... | collective-permute-start | bytes 122888 | tf_op jit(solution)/shard_map/ppermute | solution.py:30
  478.5 98.3 %collective-permute-start.45 = (f32[4,4,5,128]{3,0,2,1:T(4,128)S(1)}, f32[4,4,5,128]{3,0,2,1:T(4,128)}, u32[]{:S(2)}, u32[]{:S(2)}) collective-permute-start(f32[4,4,5,128]{3,0,2,1:T(4,128)S(1)} %maximum_maximum_fusion.5), channel_id=1, source_target_pairs={{0,7},{1,8},{2,9},{3,10},{4,11},{5,12},{6,13},{7,14},{8,15},{9,16}... | collective-permute-start | bytes 122888 | tf_op jit(solution)/shard_map/ppermute | solution.py:30
  484.1 97.8 %collective-permute-start.46 = (f32[4,4,5,128]{3,0,2,1:T(4,128)S(1)}, f32[4,4,5,128]{3,0,2,1:T(4,128)}, u32[]{:S(2)}, u32[]{:S(2)}) collective-permute-start(f32[4,4,5,128]{3,0,2,1:T(4,128)S(1)} %maximum_maximum_fusion.5), channel_id=1, source_target_pairs={{0,6},{1,7},{2,8},{3,9},{4,10},{5,11},{6,12},{7,13},{8,14},{9,15},... | collective-permute-start | bytes 122888 | tf_op jit(solution)/shard_map/ppermute | solution.py:30
  566.7 18.4 %collective-permute-start.47 = (f32[4,4,5,128]{3,0,2,1:T(4,128)S(1)}, f32[4,4,5,128]{3,0,2,1:T(4,128)S(1)}, u32[]{:S(2)}, u32[]{:S(2)}) collective-permute-start(f32[4,4,5,128]{3,0,2,1:T(4,128)S(1)} %maximum_maximum_fusion.5), channel_id=1, source_target_pairs={{0,5},{1,6},{2,7},{3,8},{4,9},{5,10},{6,11},{7,12},{8,13},{9,14},{... | collective-permute-start | bytes 122888 | tf_op jit(solution)/shard_map/ppermute | solution.py:30
  570.1 16.3 %collective-permute-start.48 = (f32[4,4,5,128]{3,0,2,1:T(4,128)S(1)}, f32[4,4,5,128]{3,0,2,1:T(4,128)S(1)}, u32[]{:S(2)}, u32[]{:S(2)}) collective-permute-start(f32[4,4,5,128]{3,0,2,1:T(4,128)S(1)} %maximum_maximum_fusion.5), channel_id=1, source_target_pairs={{0,4},{1,5},{2,6},{3,7},{4,8},{5,9},{6,10},{7,11},{8,12},{9,13},{1... | collective-permute-start | bytes 122888 | tf_op jit(solution)/shard_map/ppermute | solution.py:30
  574.7 13.1 %collective-permute-start.49 = (f32[4,4,5,128]{3,0,2,1:T(4,128)S(1)}, f32[4,4,5,128]{3,0,2,1:T(4,128)S(1)}, u32[]{:S(2)}, u32[]{:S(2)}) collective-permute-start(f32[4,4,5,128]{3,0,2,1:T(4,128)S(1)} %maximum_maximum_fusion.5), channel_id=1, source_target_pairs={{0,3},{1,4},{2,5},{3,6},{4,7},{5,8},{6,9},{7,10},{8,11},{9,12},{10... | collective-permute-start | bytes 122888 | tf_op jit(solution)/shard_map/ppermute | solution.py:30
  576.8 12.3 %collective-permute-start.50 = (f32[4,4,5,128]{3,0,2,1:T(4,128)S(1)}, f32[4,4,5,128]{3,0,2,1:T(4,128)S(1)}, u32[]{:S(2)}, u32[]{:S(2)}) collective-permute-start(f32[4,4,5,128]{3,0,2,1:T(4,128)S(1)} %maximum_maximum_fusion.5), channel_id=1, source_target_pairs={{0,2},{1,3},{2,4},{3,5},{4,6},{5,7},{6,8},{7,9},{8,10},{9,11},{10,... | collective-permute-start | bytes 122888 | tf_op jit(solution)/shard_map/ppermute | solution.py:30
  591.8 12.5 %collective-permute-start.57 = (f32[4,4,5,128]{3,0,2,1:T(4,128)S(1)}, f32[4,4,5,128]{3,0,2,1:T(4,128)S(1)}, u32[]{:S(2)}, u32[]{:S(2)}) collective-permute-start(f32[4,4,5,128]{3,0,2,1:T(4,128)S(1)} %maximum_maximum_fusion.5), channel_id=1, source_target_pairs={{6,0},{7,1},{8,2},{9,3},{10,4},{11,5},{12,6},{13,7},{14,8},{15,9},... | collective-permute-start | bytes 122888 | tf_op jit(solution)/shard_map/ppermute | solution.py:30
  595.3 13.9 %collective-permute-start.59 = (f32[4,4,5,128]{3,0,2,1:T(4,128)S(1)}, f32[4,4,5,128]{3,0,2,1:T(4,128)S(1)}, u32[]{:S(2)}, u32[]{:S(2)}) collective-permute-start(f32[4,4,5,128]{3,0,2,1:T(4,128)S(1)} %maximum_maximum_fusion.5), channel_id=1, source_target_pairs={{8,0},{9,1},{10,2},{11,3},{12,4},{13,5},{14,6},{15,7},{16,8},{17,9... | collective-permute-start | bytes 122888 | tf_op jit(solution)/shard_map/ppermute | solution.py:30
  601.2 12.4 %collective-permute-start.61 = (f32[4,4,5,128]{3,0,2,1:T(4,128)S(1)}, f32[4,4,5,128]{3,0,2,1:T(4,128)S(1)}, u32[]{:S(2)}, u32[]{:S(2)}) collective-permute-start(f32[4,4,5,128]{3,0,2,1:T(4,128)S(1)} %maximum_maximum_fusion.5), channel_id=1, source_target_pairs={{10,0},{11,1},{12,2},{13,3},{14,4},{15,5},{16,6},{17,7},{18,8},{19... | collective-permute-start | bytes 122888 | tf_op jit(solution)/shard_map/ppermute | solution.py:30
  708.2 50.7 %collective-permute-start.62 = (f32[4,4,5,128]{3,0,2,1:T(4,128)S(1)}, f32[4,4,5,128]{3,0,2,1:T(4,128)}, u32[]{:S(2)}, u32[]{:S(2)}) collective-permute-start(f32[4,4,5,128]{3,0,2,1:T(4,128)S(1)} %maximum_maximum_fusion.6), channel_id=1, source_target_pairs={{0,10},{1,11},{2,12},{3,13},{4,14},{5,15},{6,16},{7,17},{8,18},{9,... | collective-permute-start | bytes 122888 | tf_op jit(solution)/shard_map/ppermute | solution.py:30
  714.6 47.6 %collective-permute-start.63 = (f32[4,4,5,128]{3,0,2,1:T(4,128)S(1)}, f32[4,4,5,128]{3,0,2,1:T(4,128)}, u32[]{:S(2)}, u32[]{:S(2)}) collective-permute-start(f32[4,4,5,128]{3,0,2,1:T(4,128)S(1)} %maximum_maximum_fusion.6), channel_id=1, source_target_pairs={{0,9},{1,10},{2,11},{3,12},{4,13},{5,14},{6,15},{7,16},{8,17},{9,1... | collective-permute-start | bytes 122888 | tf_op jit(solution)/shard_map/ppermute | solution.py:30
  719.1 47.2 %collective-permute-start.64 = (f32[4,4,5,128]{3,0,2,1:T(4,128)S(1)}, f32[4,4,5,128]{3,0,2,1:T(4,128)}, u32[]{:S(2)}, u32[]{:S(2)}) collective-permute-start(f32[4,4,5,128]{3,0,2,1:T(4,128)S(1)} %maximum_maximum_fusion.6), channel_id=1, source_target_pairs={{0,8},{1,9},{2,10},{3,11},{4,12},{5,13},{6,14},{7,15},{8,16},{9,17... | collective-permute-start | bytes 122888 | tf_op jit(solution)/shard_map/ppermute | solution.py:30
  724.5 45.1 %collective-permute-start.65 = (f32[4,4,5,128]{3,0,2,1:T(4,128)S(1)}, f32[4,4,5,128]{3,0,2,1:T(4,128)}, u32[]{:S(2)}, u32[]{:S(2)}) collective-permute-start(f32[4,4,5,128]{3,0,2,1:T(4,128)S(1)} %maximum_maximum_fusion.6), channel_id=1, source_target_pairs={{0,7},{1,8},{2,9},{3,10},{4,11},{5,12},{6,13},{7,14},{8,15},{9,16}... | collective-permute-start | bytes 122888 | tf_op jit(solution)/shard_map/ppermute | solution.py:30
  732.0 45.3 %collective-permute-start.66 = (f32[4,4,5,128]{3,0,2,1:T(4,128)S(1)}, f32[4,4,5,128]{3,0,2,1:T(4,128)}, u32[]{:S(2)}, u32[]{:S(2)}) collective-permute-start(f32[4,4,5,128]{3,0,2,1:T(4,128)S(1)} %maximum_maximum_fusion.6), channel_id=1, source_target_pairs={{0,6},{1,7},{2,8},{3,9},{4,10},{5,11},{6,12},{7,13},{8,14},{9,15},... | collective-permute-start | bytes 122888 | tf_op jit(solution)/shard_map/ppermute | solution.py:30
  758.9 20.4 %collective-permute-start.67 = (f32[4,4,5,128]{3,0,2,1:T(4,128)S(1)}, f32[4,4,5,128]{3,0,2,1:T(4,128)S(1)}, u32[]{:S(2)}, u32[]{:S(2)}) collective-permute-start(f32[4,4,5,128]{3,0,2,1:T(4,128)S(1)} %maximum_maximum_fusion.6), channel_id=1, source_target_pairs={{0,5},{1,6},{2,7},{3,8},{4,9},{5,10},{6,11},{7,12},{8,13},{9,14},{... | collective-permute-start | bytes 122888 | tf_op jit(solution)/shard_map/ppermute | solution.py:30
  762.2 18.5 %collective-permute-start.68 = (f32[4,4,5,128]{3,0,2,1:T(4,128)S(1)}, f32[4,4,5,128]{3,0,2,1:T(4,128)S(1)}, u32[]{:S(2)}, u32[]{:S(2)}) collective-permute-start(f32[4,4,5,128]{3,0,2,1:T(4,128)S(1)} %maximum_maximum_fusion.6), channel_id=1, source_target_pairs={{0,4},{1,5},{2,6},{3,7},{4,8},{5,9},{6,10},{7,11},{8,12},{9,13},{1... | collective-permute-start | bytes 122888 | tf_op jit(solution)/shard_map/ppermute | solution.py:30
  766.3 15.8 %collective-permute-start.69 = (f32[4,4,5,128]{3,0,2,1:T(4,128)S(1)}, f32[4,4,5,128]{3,0,2,1:T(4,128)S(1)}, u32[]{:S(2)}, u32[]{:S(2)}) collective-permute-start(f32[4,4,5,128]{3,0,2,1:T(4,128)S(1)} %maximum_maximum_fusion.6), channel_id=1, source_target_pairs={{0,3},{1,4},{2,5},{3,6},{4,7},{5,8},{6,9},{7,10},{8,11},{9,12},{10... | collective-permute-start | bytes 122888 | tf_op jit(solution)/shard_map/ppermute | solution.py:30
  769.5 13.8 %collective-permute-start.70 = (f32[4,4,5,128]{3,0,2,1:T(4,128)S(1)}, f32[4,4,5,128]{3,0,2,1:T(4,128)S(1)}, u32[]{:S(2)}, u32[]{:S(2)}) collective-permute-start(f32[4,4,5,128]{3,0,2,1:T(4,128)S(1)} %maximum_maximum_fusion.6), channel_id=1, source_target_pairs={{0,2},{1,3},{2,4},{3,5},{4,6},{5,7},{6,8},{7,9},{8,10},{9,11},{10,... | collective-permute-start | bytes 122888 | tf_op jit(solution)/shard_map/ppermute | solution.py:30
  783.3 12.7 %collective-permute-start.75 = (f32[4,4,5,128]{3,0,2,1:T(4,128)S(1)}, f32[4,4,5,128]{3,0,2,1:T(4,128)S(1)}, u32[]{:S(2)}, u32[]{:S(2)}) collective-permute-start(f32[4,4,5,128]{3,0,2,1:T(4,128)S(1)} %maximum_maximum_fusion.6), channel_id=1, source_target_pairs={{4,0},{5,1},{6,2},{7,3},{8,4},{9,5},{10,6},{11,7},{12,8},{13,9},{1... | collective-permute-start | bytes 122888 | tf_op jit(solution)/shard_map/ppermute | solution.py:30
  784.7 12.8 %collective-permute-start.76 = (f32[4,4,5,128]{3,0,2,1:T(4,128)S(1)}, f32[4,4,5,128]{3,0,2,1:T(4,128)S(1)}, u32[]{:S(2)}, u32[]{:S(2)}) collective-permute-start(f32[4,4,5,128]{3,0,2,1:T(4,128)S(1)} %maximum_maximum_fusion.6), channel_id=1, source_target_pairs={{5,0},{6,1},{7,2},{8,3},{9,4},{10,5},{11,6},{12,7},{13,8},{14,9},{... | collective-permute-start | bytes 122888 | tf_op jit(solution)/shard_map/ppermute | solution.py:30
  786.0 14.4 %collective-permute-start.77 = (f32[4,4,5,128]{3,0,2,1:T(4,128)S(1)}, f32[4,4,5,128]{3,0,2,1:T(4,128)S(1)}, u32[]{:S(2)}, u32[]{:S(2)}) collective-permute-start(f32[4,4,5,128]{3,0,2,1:T(4,128)S(1)} %maximum_maximum_fusion.6), channel_id=1, source_target_pairs={{6,0},{7,1},{8,2},{9,3},{10,4},{11,5},{12,6},{13,7},{14,8},{15,9},... | collective-permute-start | bytes 122888 | tf_op jit(solution)/shard_map/ppermute | solution.py:30
  791.5 13.9 %collective-permute-start.79 = (f32[4,4,5,128]{3,0,2,1:T(4,128)S(1)}, f32[4,4,5,128]{3,0,2,1:T(4,128)S(1)}, u32[]{:S(2)}, u32[]{:S(2)}) collective-permute-start(f32[4,4,5,128]{3,0,2,1:T(4,128)S(1)} %maximum_maximum_fusion.6), channel_id=1, source_target_pairs={{8,0},{9,1},{10,2},{11,3},{12,4},{13,5},{14,6},{15,7},{16,8},{17,9... | collective-permute-start | bytes 122888 | tf_op jit(solution)/shard_map/ppermute | solution.py:30
  797.5 12.4 %collective-permute-start.81 = (f32[4,4,5,128]{3,0,2,1:T(4,128)S(1)}, f32[4,4,5,128]{3,0,2,1:T(4,128)S(1)}, u32[]{:S(2)}, u32[]{:S(2)}) collective-permute-start(f32[4,4,5,128]{3,0,2,1:T(4,128)S(1)} %maximum_maximum_fusion.6), channel_id=1, source_target_pairs={{10,0},{11,1},{12,2},{13,3},{14,4},{15,5},{16,6},{17,7},{18,8},{19... | collective-permute-start | bytes 122888 | tf_op jit(solution)/shard_map/ppermute | solution.py:30
  (219 other events, 1567.7 us)
where the time goes:
time: 985 us; the launch traced here: 971 us
  blocking collectives  291 us (30%)
  local copies, waits for them, and re-layouts  251 us (25%)
  starting transfers between devices  213 us (22%)
  other arithmetic  145 us (15%)
  waiting for transfers between devices  64.3 us (7%)
    pmax x4, blocking collectives, shards(): lax.pmax(jnp.max(jnp.where(wet_slot == 1, tile_speed(fields_now), lowest)...  291 us
    ppermute x82, starting transfers between devices, passed_along(): lax.ppermute(value, axis, [(source, source + steps) for source in range(i...  213 us
    ppermute x82, waiting for transfers between devices, passed_along(): lax.ppermute(value, axis, [(source, source + steps) for source in range(i...  64.3 us
    unnamed x467, local copies, waits for them, and re-layouts  42.4 us
    concatenate x26, local copies, waits for them, and re-layouts, north_side(): return jnp.concatenate([field[1:], ghost[None]], axis=0)  23.5 us
  transfers between devices with their start and end apart: 82, of which 36 were waited for; matrix products, arithmetic and copies ran while one was open for 9% of the time, Pallas kernels for 0%

commit v1 on v0

v1 whole, which is shorter than its diff:
```python
import functools
import math

import jax
import jax.numpy as jnp
from jax import lax
from jax.experimental import pallas as pl
from jax.experimental.pallas import tpu as pltpu
from jax.sharding import PartitionSpec as P

MESH = pl.DeviceIdType.MESH
TPD = 4
MOVE = 2
STEPS = 4
TILE = 128
BLOCKS = TILE // 8
GRAVITY = 9.81
ROOT_G = math.sqrt(GRAVITY)
SHALLOW = 0.1
COURANT = 0.45
STORAGE = 0.2
LOWEST = 2.0 * math.sqrt(GRAVITY * SHALLOW)
DEVICES = 128
F32 = jnp.float32


def peers(me):
    core = lax.rem(me, 2)
    y = lax.rem(me // 2, 4)
    z = lax.rem(me // 8, 4)
    x = me // 32
    xs = [lax.rem(x + d, 4) * 32 for d in range(4)]
    zs = [lax.rem(z + d, 4) * 8 for d in range(4)]
    ys = [lax.rem(y + d, 4) * 2 for d in range(4)]
    cs = [core, 1 - core]
    xz = [[a + b for b in zs] for a in xs]
    yc = [[a + b for b in cs] for a in ys]
    found = []
    for dx in range(4):
        for dz in range(4):
            for dy in range(4):
                for dc in range(2):
                    offset = ((dx * 4 + dz) * 4 + dy) * 2 + dc
                    if offset:
                        hops = sum(min(d, 4 - d) for d in (dx, dz, dy))
                        found.append((hops, offset, xz[dx][dz] + yc[dy][dc]))
    found.sort(key=lambda item: -item[0])
    return [(offset, target) for _, offset, target in found]


def derived(h, mx, my):
    s = jnp.maximum(h, SHALLOW)
    r = lax.rsqrt(s)
    inv = r * r
    c = (ROOT_G * s) * r
    return inv, c


def wave(h, n, inv, c):
    u = n * inv
    return u, jnp.abs(u) + c


def face(h1, n1, a1, h2, n2, a2):
    inv1, c1 = derived(h1, n1, a1)
    inv2, c2 = derived(h2, n2, a2)
    u1, w1 = wave(h1, n1, inv1, c1)
    u2, w2 = wave(h2, n2, inv2, c2)
    speed = jnp.maximum(w1, w2)
    half_g = 0.5 * GRAVITY
    mass = (n1 + n2) - speed * (h2 - h1)
    push = (n1 * u1 + half_g * h1 * h1 + n2 * u2 + half_g * h2 * h2) - speed * (n2 - n1)
    carry = (a1 * u1 + a2 * u2) - speed * (a2 - a1)
    return mass, push, carry


def flood_kernel(
    wet_ref, link_ref, dest_ref, depth_in, vel_in, head_in, terr_in, leak_in, diff_in,
    pool_out,
    U, D, R, G, L, S, KX, KY, VEL, mbuf, ew_own, ew_got, ns_own, ns_got, movers,
    in_sem, mx_send, mx_recv, ew_send, ew_recv, ns_send, ns_recv, mv_send, mv_recv, out_sem,
):
    me = lax.axis_index("tiles")
    row = me // 4
    col = lax.rem(me, 4)
    odd = lax.rem(row, 2)
    place = col + odd * (3 - 2 * col)
    base = me * TPD

    def device_at(r, c):
        o = lax.rem(r, 2)
        return r * 4 + c + o * (3 - 2 * c)

    east = device_at(row, lax.rem(place + 1, 4))
    west = device_at(row, lax.rem(place + 3, 4))
    north = device_at(lax.rem(row + 1, 32), place)
    south = device_at(lax.rem(row + 31, 32), place)
    after = lax.rem(me + 1, DEVICES)
    before = lax.rem(me + DEVICES - 1, DEVICES)
    everyone = peers(me)
    slot = [p + odd * (3 - 2 * p) for p in range(TPD)]

    loads = []
    for p in range(TPD):
        t = slot[p]
        loads.append(pltpu.make_async_copy(depth_in.at[t], U.at[p, 0], in_sem.at[0, p]))
        loads.append(pltpu.make_async_copy(vel_in.at[t], VEL.at[p], in_sem.at[1, p]))
        loads.append(pltpu.make_async_copy(head_in.at[t], U.at[p, 3], in_sem.at[2, p]))
        loads.append(pltpu.make_async_copy(terr_in.at[t], G.at[p], in_sem.at[3, p]))
        loads.append(pltpu.make_async_copy(leak_in.at[t], L.at[p], in_sem.at[4, p]))
        loads.append(pltpu.make_async_copy(diff_in.at[t], S.at[p], in_sem.at[5, p]))
    for load in loads:
        load.start()

    barrier = pltpu.get_barrier_semaphore()
    for _, target in everyone:
        pl.semaphore_signal(barrier, inc=1, device_id=(target,), device_id_type=MESH)

    wet = [wet_ref[base + slot[p]] for p in range(TPD)]
    linked = [[link_ref[k, base + slot[p]] for k in range(4)] for p in range(TPD)]
    lane = lax.broadcasted_iota(jnp.int32, (8, TILE), 1)
    sub = lax.broadcasted_iota(jnp.int32, (8, TILE), 0)
    first_lane = lane == 0
    last_lane = lane == TILE - 1
    wall_lane = [jnp.where(linked[p][1] >= 0, -1, TILE - 1) for p in range(TPD - 1)]
    wall_back = [jnp.where(linked[p][0] >= 0, -1, 0) for p in range(TPD)]
    zero = jnp.zeros((8, TILE), F32)

    def rows_of(i):
        return pl.ds(pl.multiple_of(i * 8, 8), 8)

    def pack(i, q, value, acc, edge):
        lane_at = q * BLOCKS + i
        shift = lane_at + (1 if edge else 0)
        return jnp.where(lane == lane_at, pltpu.roll(value, shift, 1), acc)

    for load in loads:
        load.wait()

    def ground_block(i, carry):
        acc_e, acc_w = carry
        blk = rows_of(i)
        acc_e = pack(i, 4, G[TPD - 1, blk, :], acc_e, True)
        acc_w = pack(i, 4, G[0, blk, :], acc_w, False)
        return acc_e, acc_w

    ground_e, ground_w = lax.fori_loop(0, BLOCKS, ground_block, (zero, zero))
    for s in range(STEPS):
        for p in range(TPD):
            ns_own[s, 0, 16 + p : 17 + p, :] = G[p, TILE - 1 : TILE, :]
            ns_own[s, 1, 16 + p : 17 + p, :] = G[p, 0:1, :]
        for k in range(2):
            ns_own[s, k, 20:24, :] = jnp.zeros((4, TILE), F32)

    def sweep(step, dt_of):
        def block(i, carry):
            acc_e, acc_w, top = carry
            blk = rows_of(i)
            top = list(top)
            for p in range(TPD):
                if dt_of is None:
                    h = U[p, 0, blk, :]
                    mx = h * VEL[p, 0, blk, :]
                    my = h * VEL[p, 1, blk, :]
                    hd = U[p, 3, blk, :]
                    U[p, 1, blk, :] = mx
                    U[p, 2, blk, :] = my
                else:
                    new = [U[p, q, blk, :] + dt_of[p] * R[p, q, blk, :] for q in range(4)]
                    for q in range(4):
                        U[p, q, blk, :] = new[q]
                    h, mx, my, hd = new
                inv, c = derived(h, mx, my)
                top[p] = jnp.maximum(top[p], (jnp.abs(mx) + jnp.abs(my)) * inv + 2.0 * c)
                if p == TPD - 1:
                    for q, value in enumerate((h, mx, my, hd)):
                        acc_e = pack(i, q, value, acc_e, True)
                if p == 0:
                    for q, value in enumerate((h, mx, my, hd)):
                        acc_w = pack(i, q, value, acc_w, False)
            return acc_e, acc_w, tuple(top)

        acc_e, acc_w, top = lax.fori_loop(
            0, BLOCKS, block, (ground_e, ground_w, (zero,) * TPD)
        )
        ew_own[step, 0] = acc_e
        ew_own[step, 1] = acc_w
        largest = jnp.full((8, TILE), LOWEST, F32)
        for p in range(TPD):
            largest = jnp.maximum(largest, jnp.where(wet[p] == 1, top[p], LOWEST))
        mbuf[step, 0:1, :] = jnp.max(largest, axis=0, keepdims=True)
        for q in range(4):
            for p in range(TPD):
                at = q * 4 + p
                ns_own[step, 0, at : at + 1, :] = U[p, q, TILE - 1 : TILE, :]
                ns_own[step, 1, at : at + 1, :] = U[p, q, 0:1, :]

    def halos(step):
        return [
            pltpu.make_async_remote_copy(
                ew_own.at[step, 0], ew_got.at[step, 1], ew_send.at[step, 0], ew_recv.at[step, 1],
                device_id=(east,), device_id_type=MESH),
            pltpu.make_async_remote_copy(
                ew_own.at[step, 1], ew_got.at[step, 0], ew_send.at[step, 1], ew_recv.at[step, 0],
                device_id=(west,), device_id_type=MESH),
            pltpu.make_async_remote_copy(
                ns_own.at[step, 0], ns_got.at[step, 1], ns_send.at[step, 0], ns_recv.at[step, 1],
                device_id=(north,), device_id_type=MESH),
            pltpu.make_async_remote_copy(
                ns_own.at[step, 1], ns_got.at[step, 0], ns_send.at[step, 1], ns_recv.at[step, 0],
                device_id=(south,), device_id_type=MESH),
        ]

    def send(step):
        for n, (offset, target) in enumerate(everyone):
            if n == 14:
                for copy in halos(step):
                    copy.start()
            pltpu.make_async_remote_copy(
                mbuf.at[step, 0:1], mbuf.at[step, offset : offset + 1],
                mx_send.at[step], mx_recv.at[step],
                device_id=(target,), device_id_type=MESH).start()

    def all_rows(step, sem):
        rest = mbuf.at[step, 1:DEVICES]
        return pltpu.make_async_copy(rest, rest, sem.at[step])

    def ground_slopes():
        def block(i, below):
            blk = rows_of(i)
            nxt = rows_of(jnp.minimum(i + 1, BLOCKS - 1))
            top_row = jnp.where(i == BLOCKS - 1, 7, -1)
            here = [G[p, blk, :] for p in range(TPD)]
            turned = [pltpu.roll(g, TILE - 1, 1) for g in here]
            back = zero
            new_below = []
            for p in range(TPD):
                g = here[p]
                if p < TPD - 1:
                    de = jnp.where(last_lane, turned[p + 1], turned[p]) - g
                    de = jnp.where(lane == wall_lane[p], 0.0, de)
                else:
                    de = jnp.where(last_lane, 0.0, turned[p] - g)
                round_de = pltpu.roll(de, 1, 1)
                dw = jnp.where(first_lane, back, round_de)
                back = round_de
                KX[p, blk, :] = (0.5 * GRAVITY) * (de + dw)
                up = jnp.where(sub == 7, pltpu.roll(G[p, nxt, :], 7, 0), pltpu.roll(g, 7, 0))
                dn = jnp.where(sub == top_row, 0.0, up - g)
                round_dn = pltpu.roll(dn, 1, 0)
                ds = jnp.where(sub == 0, below[p], round_dn)
                new_below.append(round_dn)
                KY[p, blk, :] = (0.5 * GRAVITY) * (dn + ds)
            return tuple(new_below)

        lax.fori_loop(0, BLOCKS, block, (zero,) * TPD)

    def right_sides():
        def derive(i, _):
            blk = rows_of(i)
            for p in range(TPD):
                h, mx, my = (U[p, q, blk, :] for q in range(3))
                inv, c = derived(h, mx, my)
                u, au = wave(h, mx, inv, c)
                v, av = wave(h, my, inv, c)
                still = (0.5 * GRAVITY) * h * h
                D[p, 0, blk, :] = au
                D[p, 1, blk, :] = av
                D[p, 2, blk, :] = mx * u + still
                D[p, 3, blk, :] = mx * v
                D[p, 4, blk, :] = my * v + still
            return 0

        lax.fori_loop(0, BLOCKS, derive, 0)

        def block(i, below):
            blk = rows_of(i)
            nxt = rows_of(jnp.minimum(i + 1, BLOCKS - 1))
            top_row = jnp.where(i == BLOCKS - 1, 7, -1)
            new_below = []
            after_turned = None
            east_faces = [None] * TPD
            sides = [None] * TPD
            for p in reversed(range(TPD)):
                h, mx, my, hd = (U[p, q, blk, :] for q in range(4))
                au, fxx, fxy = D[p, 0, blk, :], D[p, 2, blk, :], D[p, 3, blk, :]
                own = (h, mx, my, hd, au, fxx, fxy)
                turned = [pltpu.roll(value, TILE - 1, 1) for value in own]
                if after_turned is None:
                    he, me_, ye, de, ae, xe, ce = turned
                else:
                    he, me_, ye, de, ae, xe, ce = (
                        jnp.where(last_lane, b, a) for a, b in zip(turned, after_turned)
                    )
                after_turned = turned
                speed = jnp.maximum(au, ae)
                g0 = (mx + me_) - speed * (he - h)
                g1 = (fxx + xe) - speed * (me_ - mx)
                g2 = (fxy + ce) - speed * (ye - my)
                g3 = de - hd
                step_out = au * mx
                if p == TPD - 1:
                    wall, push = last_lane, 0.0
                else:
                    wall, push = lane == wall_lane[p], 2.0 * (fxx + step_out)
                g0 = jnp.where(wall, 0.0, g0)
                g1 = jnp.where(wall, push, g1)
                g2 = jnp.where(wall, 0.0, g2)
                g3 = jnp.where(wall, 0.0, g3)
                east_faces[p] = (g0, g1, g2, g3)
                sides[p] = 2.0 * (fxx - step_out)
            back = (zero,) * 4
            for p in range(TPD):
                rounds = [pltpu.roll(g, 1, 1) for g in east_faces[p]]
                west_faces = [jnp.where(first_lane, b, a) for a, b in zip(rounds, back)]
                if p > 0:
                    west_faces[1] = jnp.where(lane == wall_back[p], sides[p], west_faces[1])
                back = rounds
                x0, x1, x2, x3 = (e - w for e, w in zip(east_faces[p], west_faces))

                h, mx, my, hd = (U[p, q, blk, :] for q in range(4))
                av, fxy, fyy = D[p, 1, blk, :], D[p, 3, blk, :], D[p, 4, blk, :]
                own = (h, mx, my, hd, av, fxy, fyy)
                ups = (U[p, 0, nxt, :], U[p, 1, nxt, :], U[p, 2, nxt, :], U[p, 3, nxt, :],
                       D[p, 1, nxt, :], D[p, 3, nxt, :], D[p, 4, nxt, :])
                hn, xn, mn, dn, an, cn, yn = (
                    jnp.where(sub == 7, pltpu.roll(b, 7, 0), pltpu.roll(a, 7, 0))
                    for a, b in zip(own, ups)
                )
                speed = jnp.maximum(av, an)
                f0 = (my + mn) - speed * (hn - h)
                f1 = (fyy + yn) - speed * (mn - my)
                f2 = (fxy + cn) - speed * (xn - mx)
                f3 = dn - hd
                faces = [jnp.where(sub == top_row, 0.0, f) for f in (f0, f1, f2, f3)]
                rounds = [pltpu.roll(f, 1, 0) for f in faces]
                lower = [jnp.where(sub == 0, b, a) for a, b in zip(rounds, below[4 * p : 4 * p + 4])]
                new_below.extend(rounds)
                y0, y1, y2, y3 = (n - s for n, s in zip(faces, lower))

                seep = L[p, blk, :] * (h + G[p, blk, :] - hd)
                R[p, 0, blk, :] = -0.5 * (x0 + y0) - seep
                R[p, 1, blk, :] = -0.5 * (x1 + y2) - h * KX[p, blk, :]
                R[p, 2, blk, :] = -0.5 * (x2 + y1) - h * KY[p, blk, :]
                R[p, 3, blk, :] = S[p, blk, :] * (x3 + y3) + seep * (1.0 / STORAGE)
            return tuple(new_below)

        lax.fori_loop(0, BLOCKS, block, (zero,) * (4 * TPD))

    def column_terms(own, got, link, flip_east):
        ghost = jnp.where(link >= 0, got, jnp.where(lane // BLOCKS == 1, -own, own))
        part = lambda packed, q: packed if q == 0 else pltpu.roll(packed, TILE - q * BLOCKS, 1)
        h, n, a, hd, g = (part(own, q) for q in range(5))
        gh, gn, ga, ghd, gg = (part(ghost, q) for q in range(5))
        if flip_east:
            mass, push, carry = face(h, n, a, gh, gn, ga)
            sign = -0.5
        else:
            mass, push, carry = face(gh, gn, ga, h, n, a)
            sign = 0.5
        slope = (0.5 * GRAVITY) * h * ((gg - g) if flip_east else (g - gg))
        return sign * mass, sign * push - slope, sign * carry, ghd - hd

    def row_terms(own, got, k, is_north):
        rows = lax.broadcasted_iota(jnp.int32, (TPD, TILE), 0)
        link = jnp.full((TPD, TILE), linked[0][k], jnp.int32)
        for p in range(1, TPD):
            link = jnp.where(rows == p, linked[p][k], link)
        mine = [own[q * 4 : q * 4 + 4, :] for q in range(5)]
        signs = (1.0, 1.0, -1.0, 1.0, 1.0)
        ghost = [
            jnp.where(link >= 0, got[q * 4 : q * 4 + 4, :], signs[q] * mine[q]) for q in range(5)
        ]
        h, a, n, hd, g = mine
        gh, ga, gn, ghd, gg = ghost
        if is_north:
            mass, push, carry = face(h, n, a, gh, gn, ga)
            sign = -0.5
        else:
            mass, push, carry = face(gh, gn, ga, h, n, a)
            sign = 0.5
        slope = (0.5 * GRAVITY) * h * ((gg - g) if is_north else (g - gg))
        return sign * mass, sign * carry, sign * push - slope, ghd - hd

    def rims(step):
        for copy in halos(step):
            copy.wait_recv()
        for side, p, edge in ((0, TPD - 1, True), (1, 0, False)):
            terms = column_terms(
                ew_own[step, side], ew_got[step, side], linked[p][1 - side], edge
            )
            at_edge = last_lane if edge else first_lane

            def block(i, _):
                blk = rows_of(i)
                shift = (TILE - 1 - i) if edge else lax.rem(TILE - i, TILE)
                for q in range(4):
                    add = pltpu.roll(terms[q], shift, 1)
                    if q == 3:
                        add = add * S[p, blk, :]
                    R[p, q, blk, :] += jnp.where(at_edge, add, 0.0)
                return 0

            lax.fori_loop(0, BLOCKS, block, 0)
        for side, at in ((0, TILE - 1), (1, 0)):
            terms = row_terms(ns_own.at[step, side], ns_got.at[step, side], 3 - side, side == 0)
            for p in range(TPD):
                for q in range(4):
                    add = terms[q][p : p + 1, :]
                    if q == 3:
                        add = add * S[p, at : at + 1, :]
                    R[p, q, at : at + 1, :] += add

    def interval(step):
        all_rows(step, mx_recv).wait()
        top = jnp.max(jnp.max(mbuf[step], axis=0, keepdims=True), axis=1, keepdims=True)
        dt = COURANT / jnp.broadcast_to(top, (8, TILE))
        return [jnp.where(wet[p] == 1, dt, 0.0) for p in range(TPD)]

    sweep(0, None)
    pl.semaphore_wait(barrier, DEVICES - 1)

    def body(step, _):
        send(step)
        right_sides()
        rims(step)
        sweep(step + 1, interval(step))
        return 0

    send(0)
    ground_slopes()
    right_sides()
    rims(0)
    sweep(1, interval(0))
    lax.fori_loop(1, STEPS, body, 0)

    def movers_of(flags):
        count = jnp.int32(0)
        picks = [jnp.int32(0), jnp.int32(0)]
        for t in range(TPD):
            at = t + odd * (3 - 2 * t)
            for j in range(MOVE):
                picks[j] = jnp.where(jnp.logical_and(flags[t], count == j), at, picks[j])
            count = count + flags[t].astype(jnp.int32)
        return picks

    targets_of = [dest_ref[base + t] for t in range(TPD)]
    rightward = movers_of([d >= base + TPD for d in targets_of])
    leftward = movers_of([d < base for d in targets_of])
    keep = pltpu.make_async_copy(U.at[:, 0:4], pool_out.at[0:TPD], out_sem.at[0])
    keep.start()
    sent = []
    for j in range(MOVE):
        for side, picks, target in ((0, rightward, after), (1, leftward, before)):
            for q in range(4):
                movers[side, j, q] = U[picks[j], q]
            copy = pltpu.make_async_remote_copy(
                movers.at[side, j], pool_out.at[TPD + side * MOVE + j],
                mv_send.at[side, j], mv_recv.at[side, j],
                device_id=(target,), device_id_type=MESH)
            copy.start()
            sent.append(copy)
    for step in range(STEPS):
        all_rows(step, mx_send).wait()
        for copy in halos(step):
            copy.wait_send()
    keep.wait()
    for copy in sent:
        copy.wait()


def pick_kernel(dest_ref, pool, depth_out, flow_out, head_out, sem):
    me = lax.axis_index("tiles")
    base = me * TPD
    last = DEVICES - 1

    def odd_of(device):
        return lax.rem(device // 4, 2)

    wanted = [jnp.int32(0)] * TPD
    odd = odd_of(me)
    for t in range(TPD):
        d = dest_ref[base + t]
        at = t + odd * (3 - 2 * t)
        for k in range(TPD):
            wanted[k] = jnp.where(d == base + k, at, wanted[k])
    rank = jnp.int32(0)
    for t in range(TPD):
        d = dest_ref[jnp.maximum(base - TPD, 0) + t]
        came = jnp.logical_and(d >= base, me > 0)
        for k in range(TPD):
            wanted[k] = jnp.where(jnp.logical_and(came, d == base + k), TPD + rank, wanted[k])
        rank = rank + came.astype(jnp.int32)
    rank = jnp.int32(0)
    for t in range(TPD):
        d = dest_ref[jnp.minimum(base + TPD, last * TPD) + t]
        came = jnp.logical_and(d < base + TPD, me < last)
        for k in range(TPD):
            wanted[k] = jnp.where(
                jnp.logical_and(came, d == base + k), TPD + MOVE + rank, wanted[k]
            )
        rank = rank + came.astype(jnp.int32)
    copies = []
    for k in range(TPD):
        w = wanted[k]
        copies.append(pltpu.make_async_copy(pool.at[w, 0], depth_out.at[k], sem.at[0, k]))
        copies.append(pltpu.make_async_copy(pool.at[w, 1:3], flow_out.at[k], sem.at[1, k]))
        copies.append(pltpu.make_async_copy(pool.at[w, 3], head_out.at[k], sem.at[2, k]))
    for copy in copies:
        copy.start()
    for copy in copies:
        copy.wait()


def shards(depth, velocity, head, terrain, leakance, diffusivity, tile_wet, neighbours, destination):
    hbm = pl.BlockSpec(memory_space=pltpu.HBM)
    vmem = pl.BlockSpec(memory_space=pltpu.VMEM)
    smem = pl.BlockSpec(memory_space=pltpu.SMEM)
    vm = lambda *shape: pltpu.VMEM(shape + (TILE,), F32)
    dma = pltpu.SemaphoreType.DMA
    pool = pl.pallas_call(
        flood_kernel,
        out_shape=jax.ShapeDtypeStruct((TPD + 2 * MOVE, 4, TILE, TILE), F32),
        in_specs=[smem] * 3 + [hbm] * 6,
        out_specs=vmem,
        scratch_shapes=[
            vm(TPD, 4, TILE), vm(TPD, 5, TILE), vm(TPD, 4, TILE),
            vm(TPD, TILE), vm(TPD, TILE), vm(TPD, TILE), vm(TPD, TILE), vm(TPD, TILE),
            vm(TPD, 2, TILE), vm(STEPS + 1, DEVICES),
            vm(STEPS + 1, 2, 8), vm(STEPS, 2, 8), vm(STEPS + 1, 2, 24), vm(STEPS, 2, 24),
            vm(2, MOVE, 4, TILE),
            dma((6, TPD)), dma((STEPS,)), dma((STEPS,)),
            dma((STEPS, 2)), dma((STEPS, 2)), dma((STEPS, 2)), dma((STEPS, 2)),
            dma((2, MOVE)), dma((2, MOVE)), dma((1,)),
        ],
        compiler_params=pltpu.CompilerParams(
            collective_id=0, has_side_effects=True, vmem_limit_bytes=60 << 20
        ),
    )(tile_wet, neighbours.T, destination, depth, velocity, head, terrain, leakance, diffusivity)
    tile = jax.ShapeDtypeStruct((TPD, TILE, TILE), F32)
    return pl.pallas_call(
        pick_kernel,
        out_shape=(tile, jax.ShapeDtypeStruct((TPD, 2, TILE, TILE), F32), tile),
        in_specs=[smem, vmem],
        out_specs=(hbm,) * 3,
        scratch_shapes=[dma((3, TPD))],
    )(destination, pool)


def solution(mesh):
    tiles = P("tiles", None, None)
    pair = P("tiles", None, None, None)
    return jax.shard_map(
        shards,
        mesh=mesh,
        in_specs=(tiles, pair, tiles, tiles, tiles, tiles, P(), P(), P()),
        out_specs=(tiles, pair, tiles),
        check_vma=False,
    )
```

time: 985 us -> 65 us (0.07); the launches traced: 971 us -> 64.8 us
  blocking collectives: 291 us -> 0 us
  local copies, waits for them, and re-layouts: 251 us -> 0 us
  starting transfers between devices: 213 us -> 0 us
  other arithmetic: 145 us -> 0 us
  waiting for transfers between devices: 64.3 us -> 0 us
  Pallas kernels: 0 us -> 64.1 us
    pmax x4 -> x0, blocking collectives: 291 us -> none  [shards(): lax.pmax(jnp.max(jnp.where(wet_slot == 1, tile_speed(fields_now), lowest)...]
    ppermute x82 -> x0, starting transfers between devices: 213 us -> none  [passed_along(): lax.ppermute(value, axis, [(source, source + steps) for source in range(i...]
    ppermute x82 -> x0, waiting for transfers between devices: 64.3 us -> none  [passed_along(): lax.ppermute(value, axis, [(source, source + steps) for source in range(i...]
    pallas_call x0 -> x2, Pallas kernels: none -> 64.1 us  [the longest x1 61.4 us: shards(): pl.pallas_call(flood_kernel, out_shape=jax.ShapeDtypeStruct((TPD + 2 * MO...]
    concatenate x79 -> x0, local copies, waits for them, and re-layouts: 61.3 us -> none  [the longest x26 23.5 us: north_side(): return jnp.concatenate([field[1:], ghost[None]], axis=0)]
    sub x22 -> x0, other arithmetic: 44.3 us -> none  [the longest x5 10 us: advance(): east_flow - interval * (flux_east[1] - flux_west[1] + (flux_north[2] - fl...]
    concatenate x37 -> x0, other arithmetic: 43.4 us -> none  [the longest x7 12.6 us: advance(): jnp.concatenate([rim_south[part_index][None], flux_north[part_index][:-1]...]
    unnamed x467 -> x0, local copies, waits for them, and re-layouts: 42.4 us -> none
  transfers between devices with their start and end apart: 82 -> 0, of which waited for: 36 -> 0; matrix products, arithmetic and copies ran while one was open for 9% -> 0% of each run, Pallas kernels for 0% -> 0%
where the time goes in v1:
time: 65 us; the launch traced here: 64.8 us
  Pallas kernels  64.1 us (99%)
    pallas_call x1, Pallas kernels, shards(): pl.pallas_call(flood_kernel, out_shape=jax.ShapeDtypeStruct((TPD + 2 * MO...  61.4 us
    pallas_call x1, Pallas kernels, shards(): pl.pallas_call(pick_kernel, out_shape=(tile, jax.ShapeDtypeStruct((TPD, 2...  2.72 us

profile of v1, /device:TPU:0, one launch (start us, length us, event | category | flops | bytes accessed | tf_op | source)
XLA Modules:
  0.0 64.8 jit_solution(17708928940930746574)
XLA Ops:
  0.6 61.4 %shard_map.112.pool = f32[8,4,128,128]{3,2,1,0:T(8,128)} custom-call(s32[512]{0:T(512)} %wet_ref.1, s32[4,512]{1,0:T(4,128)} %bitcast.1, s32[512]{0:T(512)} %dest_ref.3, f32[4,128,128]{2,1,0:T(8,128)} %depth_in.1, f32[4,2,128,128]{3,2,1,0:T(8,128)} %vel_in.1, f32[4,128,128]{2,1,0:T(8,128)} %head_in.1, f32[4,128,128]{2,1,0:T(8,128)} %terr_in.1, ...), custom_call_target="tpu_custom_call" | custom-call | tf_op jit(solution)/shard_map/pallas_call | solution.py:521
  62.0 2.7 %shard_map.113 = (f32[4,128,128]{2,1,0:T(8,128)}, f32[4,2,128,128]{3,2,1,0:T(8,128)}, f32[4,128,128]{2,1,0:T(8,128)}) custom-call(s32[512]{0:T(512)} %dest_ref.3, f32[8,4,128,128]{3,2,1,0:T(8,128)} %shard_map.112.pool), custom_call_target="tpu_custom_call" | custom-call | tf_op jit(solution)/shard_map/pallas_call | solution.py:541

commit v2 on v1

--- a/solution.py
+++ b/solution.py
@@ -127,11 +127,11 @@
     zero = jnp.zeros((8, TILE), F32)
 
     def rows_of(i):
-        return pl.ds(pl.multiple_of(i * 8, 8), 8)
+        return pl.ds(i * 8 if isinstance(i, int) else pl.multiple_of(i * 8, 8), 8)
 
     def pack(i, q, value, acc, edge):
         lane_at = q * BLOCKS + i
-        shift = lane_at + (1 if edge else 0)
+        shift = (lane_at + (1 if edge else 0)) % TILE
         return jnp.where(lane == lane_at, pltpu.roll(value, shift, 1), acc)
 
     for load in loads:
@@ -144,7 +144,9 @@
         acc_w = pack(i, 4, G[0, blk, :], acc_w, False)
         return acc_e, acc_w
 
-    ground_e, ground_w = lax.fori_loop(0, BLOCKS, ground_block, (zero, zero))
+    ground_e = ground_w = zero
+    for i in range(BLOCKS):
+        ground_e, ground_w = ground_block(i, (ground_e, ground_w))
     for s in range(STEPS):
         for p in range(TPD):
             ns_own[s, 0, 16 + p : 17 + p, :] = G[p, TILE - 1 : TILE, :]
@@ -180,9 +182,10 @@
                         acc_w = pack(i, q, value, acc_w, False)
             return acc_e, acc_w, tuple(top)
 
-        acc_e, acc_w, top = lax.fori_loop(
-            0, BLOCKS, block, (ground_e, ground_w, (zero,) * TPD)
-        )
+        state = (ground_e, ground_w, (zero,) * TPD)
+        for i in range(BLOCKS):
+            state = block(i, state)
+        acc_e, acc_w, top = state
         ew_own[step, 0] = acc_e
         ew_own[step, 1] = acc_w
         largest = jnp.full((8, TILE), LOWEST, F32)
@@ -213,7 +216,7 @@
 
     def send(step):
         for n, (offset, target) in enumerate(everyone):
-            if n == 14:
+            if n == 2:
                 for copy in halos(step):
                     copy.start()
             pltpu.make_async_remote_copy(
@@ -271,7 +274,7 @@
                 D[p, 4, blk, :] = my * v + still
             return 0
 
-        lax.fori_loop(0, BLOCKS, derive, 0)
+        lax.fori_loop(0, BLOCKS, derive, 0, unroll=4)
 
         def block(i, below):
             blk = rows_of(i)
@@ -345,7 +348,7 @@
                 R[p, 3, blk, :] = S[p, blk, :] * (x3 + y3) + seep * (1.0 / STORAGE)
             return tuple(new_below)
 
-        lax.fori_loop(0, BLOCKS, block, (zero,) * (4 * TPD))
+        lax.fori_loop(0, BLOCKS, block, (zero,) * (4 * TPD), unroll=2)
 
     def column_terms(own, got, link, flip_east):
         ghost = jnp.where(link >= 0, got, jnp.where(lane // BLOCKS == 1, -own, own))
@@ -391,17 +394,14 @@
             )
             at_edge = last_lane if edge else first_lane
 
-            def block(i, _):
+            for i in range(BLOCKS):
                 blk = rows_of(i)
-                shift = (TILE - 1 - i) if edge else lax.rem(TILE - i, TILE)
+                shift = (TILE - 1 - i) if edge else (TILE - i) % TILE
                 for q in range(4):
                     add = pltpu.roll(terms[q], shift, 1)
                     if q == 3:
                         add = add * S[p, blk, :]
                     R[p, q, blk, :] += jnp.where(at_edge, add, 0.0)
-                return 0
-
-            lax.fori_loop(0, BLOCKS, block, 0)
         for side, at in ((0, TILE - 1), (1, 0)):
             terms = row_terms(ns_own.at[step, side], ns_got.at[step, side], 3 - side, side == 0)
             for p in range(TPD):
@@ -418,6 +418,7 @@
         return [jnp.where(wet[p] == 1, dt, 0.0) for p in range(TPD)]
 
     sweep(0, None)
+    ground_slopes()
     pl.semaphore_wait(barrier, DEVICES - 1)
 
     def body(step, _):
@@ -427,12 +428,7 @@
         sweep(step + 1, interval(step))
         return 0
 
-    send(0)
-    ground_slopes()
-    right_sides()
-    rims(0)
-    sweep(1, interval(0))
-    lax.fori_loop(1, STEPS, body, 0)
+    lax.fori_loop(0, STEPS, body, 0)
 
     def movers_of(flags):
         count = jnp.int32(0)
@@ -469,7 +465,7 @@
         copy.wait()
 
 
-def pick_kernel(dest_ref, pool, depth_out, flow_out, head_out, sem):
+def pick_kernel(dest_ref, pool, depth_out, flow_out, head_out, held, in_sem, sem):
     me = lax.axis_index("tiles")
     base = me * TPD
     last = DEVICES - 1
@@ -500,21 +496,24 @@
                 jnp.logical_and(came, d == base + k), TPD + MOVE + rank, wanted[k]
             )
         rank = rank + came.astype(jnp.int32)
+    fetches = [pltpu.make_async_copy(pool.at[wanted[k]], held.at[k], in_sem.at[k]) for k in range(TPD)]
+    for fetch in fetches:
+        fetch.start()
     copies = []
     for k in range(TPD):
-        w = wanted[k]
-        copies.append(pltpu.make_async_copy(pool.at[w, 0], depth_out.at[k], sem.at[0, k]))
-        copies.append(pltpu.make_async_copy(pool.at[w, 1:3], flow_out.at[k], sem.at[1, k]))
-        copies.append(pltpu.make_async_copy(pool.at[w, 3], head_out.at[k], sem.at[2, k]))
-    for copy in copies:
-        copy.start()
+        fetches[k].wait()
+        for n, (part, out) in enumerate(
+            ((held.at[k, 0], depth_out), (held.at[k, 1:3], flow_out), (held.at[k, 3], head_out))
+        ):
+            copy = pltpu.make_async_copy(part, out.at[k], sem.at[n, k])
+            copy.start()
+            copies.append(copy)
     for copy in copies:
         copy.wait()
 
 
 def shards(depth, velocity, head, terrain, leakance, diffusivity, tile_wet, neighbours, destination):
     hbm = pl.BlockSpec(memory_space=pltpu.HBM)
-    vmem = pl.BlockSpec(memory_space=pltpu.VMEM)
     smem = pl.BlockSpec(memory_space=pltpu.SMEM)
     vm = lambda *shape: pltpu.VMEM(shape + (TILE,), F32)
     dma = pltpu.SemaphoreType.DMA
@@ -522,7 +521,7 @@
         flood_kernel,
         out_shape=jax.ShapeDtypeStruct((TPD + 2 * MOVE, 4, TILE, TILE), F32),
         in_specs=[smem] * 3 + [hbm] * 6,
-        out_specs=vmem,
+        out_specs=hbm,
         scratch_shapes=[
             vm(TPD, 4, TILE), vm(TPD, 5, TILE), vm(TPD, 4, TILE),
             vm(TPD, TILE), vm(TPD, TILE), vm(TPD, TILE), vm(TPD, TILE), vm(TPD, TILE),
@@ -541,9 +540,9 @@
     return pl.pallas_call(
         pick_kernel,
         out_shape=(tile, jax.ShapeDtypeStruct((TPD, 2, TILE, TILE), F32), tile),
-        in_specs=[smem, vmem],
+        in_specs=[smem, hbm],
         out_specs=(hbm,) * 3,
-        scratch_shapes=[dma((3, TPD))],
+        scratch_shapes=[vm(TPD, 4, TILE), dma((TPD,)), dma((3, TPD))],
     )(destination, pool)
 
 

time: 65 us -> 49.5 us (0.76)
  Pallas kernels: 64.1 us -> 48.6 us
    pallas_call x1, Pallas kernels: 61.4 us -> 45.8 us  [shards(): pl.pallas_call(flood_kernel, out_shape=jax.ShapeDtypeStruct((TPD + 2 * MO...]
where the time goes in v2:
time: 49.5 us; the launch traced here: 49.3 us
  Pallas kernels  48.6 us (98%)
  between operations  0.64 us (1%)
    pallas_call x1, Pallas kernels, shards(): pl.pallas_call(flood_kernel, out_shape=jax.ShapeDtypeStruct((TPD + 2 * MO...  45.8 us
    pallas_call x1, Pallas kernels, shards(): pl.pallas_call(pick_kernel, out_shape=(tile, jax.ShapeDtypeStruct((TPD, 2...  2.8 us

profile of v2, /device:TPU:0, one launch (start us, length us, event | category | flops | bytes accessed | tf_op | source)
XLA Modules:
  0.0 49.3 jit_solution(8970100091614772529)
XLA Ops:
  0.6 45.8 %shard_map.112.pool = f32[8,4,128,128]{3,2,1,0:T(8,128)} custom-call(s32[512]{0:T(512)} %wet_ref.1, s32[4,512]{1,0:T(4,128)} %bitcast.1, s32[512]{0:T(512)} %dest_ref.3, f32[4,128,128]{2,1,0:T(8,128)} %depth_in.1, f32[4,2,128,128]{3,2,1,0:T(8,128)} %vel_in.1, f32[4,128,128]{2,1,0:T(8,128)} %head_in.1, f32[4,128,128]{2,1,0:T(8,128)} %terr_in.1, ...), custom_call_target="tpu_custom_call" | custom-call | tf_op jit(solution)/shard_map/pallas_call | solution.py:520
  46.5 2.8 %shard_map.113 = (f32[4,128,128]{2,1,0:T(8,128)}, f32[4,2,128,128]{3,2,1,0:T(8,128)}, f32[4,128,128]{2,1,0:T(8,128)}) custom-call(s32[512]{0:T(512)} %dest_ref.3, f32[8,4,128,128]{3,2,1,0:T(8,128)} %shard_map.112.pool), custom_call_target="tpu_custom_call" | custom-call | tf_op jit(solution)/shard_map/pallas_call | solution.py:540

commit v3 on v2

--- a/solution.py
+++ b/solution.py
@@ -76,9 +76,11 @@
 
 def flood_kernel(
     wet_ref, link_ref, dest_ref, depth_in, vel_in, head_in, terr_in, leak_in, diff_in,
-    pool_out,
-    U, D, R, G, L, S, KX, KY, VEL, mbuf, ew_own, ew_got, ns_own, ns_got, movers,
-    in_sem, mx_send, mx_recv, ew_send, ew_recv, ns_send, ns_recv, mv_send, mv_recv, out_sem,
+    tiles_out,
+    U, D, R, G, L, S, KX, KY, VEL, mbuf, ew_own, ew_got, ns_own, ns_got,
+    movers, mover_ground, arrived_ground, DA, line_own, line_got, made,
+    in_sem, mx_send, mx_recv, ew_send, ew_recv, ns_send, ns_recv, mv_send, mv_recv,
+    mg_send, mg_recv, ln_send, ln_recv, out_sem,
 ):
     me = lax.axis_index("tiles")
     row = me // 4
@@ -101,20 +103,26 @@
     slot = [p + odd * (3 - 2 * p) for p in range(TPD)]
 
     loads = []
-    for p in range(TPD):
-        t = slot[p]
-        loads.append(pltpu.make_async_copy(depth_in.at[t], U.at[p, 0], in_sem.at[0, p]))
-        loads.append(pltpu.make_async_copy(vel_in.at[t], VEL.at[p], in_sem.at[1, p]))
-        loads.append(pltpu.make_async_copy(head_in.at[t], U.at[p, 3], in_sem.at[2, p]))
-        loads.append(pltpu.make_async_copy(terr_in.at[t], G.at[p], in_sem.at[3, p]))
-        loads.append(pltpu.make_async_copy(leak_in.at[t], L.at[p], in_sem.at[4, p]))
-        loads.append(pltpu.make_async_copy(diff_in.at[t], S.at[p], in_sem.at[5, p]))
-    for load in loads:
+    for n, (array, place_of) in enumerate((
+        (depth_in, lambda p: U.at[p, 0]), (vel_in, lambda p: VEL.at[p]),
+        (head_in, lambda p: U.at[p, 3]), (terr_in, lambda p: G.at[p]),
+        (leak_in, lambda p: L.at[p]), (diff_in, lambda p: S.at[p]),
+    )):
+        for p in range(TPD):
+            loads.append(pltpu.make_async_copy(array.at[slot[p]], place_of(p), in_sem.at[n, p]))
+    early, late = loads[: 4 * TPD], loads[4 * TPD :]
+
+    barrier = pltpu.get_barrier_semaphore()
+
+    def announce(some):
+        for _, target in some:
+            pl.semaphore_signal(barrier, inc=1, device_id=(target,), device_id_type=MESH)
+
+    for load in early:
         load.start()
-
-    barrier = pltpu.get_barrier_semaphore()
-    for _, target in everyone:
-        pl.semaphore_signal(barrier, inc=1, device_id=(target,), device_id_type=MESH)
+    announce(everyone)
+    for load in late:
+        load.start()
 
     wet = [wet_ref[base + slot[p]] for p in range(TPD)]
     linked = [[link_ref[k, base + slot[p]] for k in range(4)] for p in range(TPD)]
@@ -134,7 +142,7 @@
         shift = (lane_at + (1 if edge else 0)) % TILE
         return jnp.where(lane == lane_at, pltpu.roll(value, shift, 1), acc)
 
-    for load in loads:
+    for load in early:
         load.wait()
 
     def ground_block(i, carry):
@@ -415,88 +423,271 @@
         all_rows(step, mx_recv).wait()
         top = jnp.max(jnp.max(mbuf[step], axis=0, keepdims=True), axis=1, keepdims=True)
         dt = COURANT / jnp.broadcast_to(top, (8, TILE))
-        return [jnp.where(wet[p] == 1, dt, 0.0) for p in range(TPD)]
+        return dt, [jnp.where(wet[p] == 1, dt, 0.0) for p in range(TPD)]
 
     sweep(0, None)
-    ground_slopes()
     pl.semaphore_wait(barrier, DEVICES - 1)
+
+    def ranked(flags, values):
+        count = jnp.int32(0)
+        picks = [jnp.int32(0)] * MOVE
+        for flag, value in zip(flags, values):
+            for j in range(MOVE):
+                picks[j] = jnp.where(jnp.logical_and(flag, count == j), value, picks[j])
+            count = count + flag.astype(jnp.int32)
+        return picks
+
+    mine = [dest_ref[base + t] for t in range(TPD)]
+    leaving = [
+        ranked([d >= base + TPD for d in mine], slot),
+        ranked([d < base for d in mine], slot),
+    ]
+    wanted = [jnp.int32(0)] * TPD
+    wanted_wet = [jnp.int32(0)] * TPD
+
+    def offer(flag, goes, tile, tile_wet):
+        for k in range(TPD):
+            here = jnp.logical_and(flag, goes == base + k)
+            wanted[k] = jnp.where(here, tile, wanted[k])
+            wanted_wet[k] = jnp.where(here, tile_wet, wanted_wet[k])
+
+    for t in range(TPD):
+        offer(mine[t] >= base, mine[t], slot[t], wet_ref[base + t])
+    for first_slot, side, reach in ((before * TPD, 0, me > 0), (after * TPD, 1, me < DEVICES - 1)):
+        rank = jnp.int32(0)
+        for t in range(TPD):
+            goes = dest_ref[first_slot + t]
+            comes = goes >= base if side == 0 else goes < base + TPD
+            comes = jnp.logical_and(reach, comes)
+            tile = TPD + side * MOVE + jnp.minimum(rank, MOVE - 1)
+            offer(comes, goes, tile, wet_ref[first_slot + t])
+            rank = rank + comes.astype(jnp.int32)
+
+    def grounds(kind):
+        return [
+            pltpu.make_async_remote_copy(
+                mover_ground.at[side, kind], arrived_ground.at[side, kind],
+                mg_send.at[side, kind], mg_recv.at[side, kind],
+                device_id=(target,), device_id_type=MESH)
+            for side, target in ((0, after), (1, before))
+        ]
+
+    PIECES = ((0, 0, TILE), (1, 0, TILE // 2), (1, TILE // 2, TILE // 2))
+
+    def fields_of(piece):
+        j, start, count = PIECES[piece]
+        rows = pl.ds(start, count)
+        return [
+            pltpu.make_async_remote_copy(
+                movers.at[side, j, :, rows, :], U.at[TPD + side * MOVE + j, :, rows, :],
+                mv_send.at[side, piece], mv_recv.at[side, piece],
+                device_id=(target,), device_id_type=MESH)
+            for side, target in ((0, after), (1, before))
+        ]
+
+    def lines():
+        return [
+            pltpu.make_async_remote_copy(
+                line_own.at[side], line_got.at[side], ln_send.at[side], ln_recv.at[side],
+                device_id=(target,), device_id_type=MESH)
+            for side, target in ((0, after), (1, before))
+        ]
+
+    def outer_lines():
+        for side in range(2):
+            for j in range(MOVE):
+                tile = leaving[side][j]
+                acc = zero
+                for q in range(4):
+                    line_own[side, j, q : q + 1, :] = R[tile, q, TILE - 1 : TILE, :]
+                    line_own[side, j, 4 + q : 5 + q, :] = R[tile, q, 0:1, :]
+                    for i in range(BLOCKS):
+                        value = R[tile, q, rows_of(i), :]
+                        at = q * BLOCKS + i
+                        acc = jnp.where(lane == at, pltpu.roll(value, at, 1), acc)
+                        at += TILE // 2
+                        acc = jnp.where(lane == at, pltpu.roll(value, (at + 1) % TILE, 1), acc)
+                line_own[side, j, 8:16, :] = acc
+
+    def arrived_sides(j):
+        def derive(i, _):
+            blk = rows_of(i)
+            for side in range(2):
+                h, mx, my = (U[TPD + side * MOVE + j, q, blk, :] for q in range(3))
+                inv, c = derived(h, mx, my)
+                u, au = wave(h, mx, inv, c)
+                v, av = wave(h, my, inv, c)
+                still = (0.5 * GRAVITY) * h * h
+                DA[side, 0, blk, :] = au
+                DA[side, 1, blk, :] = av
+                DA[side, 2, blk, :] = mx * u + still
+                DA[side, 3, blk, :] = mx * v
+                DA[side, 4, blk, :] = my * v + still
+            return 0
+
+
+        def block(i, below):
+            blk = rows_of(i)
+            nxt = rows_of(jnp.minimum(i + 1, BLOCKS - 1))
+            new_below = []
+            for side in range(2):
+                old = below[5 * side : 5 * side + 5]
+                h, mx, my, hd = (U[TPD + side * MOVE + j, q, blk, :] for q in range(4))
+                g = arrived_ground[side, 0, j, blk, :]
+                au, av, fxx, fxy, fyy = (DA[side, n, blk, :] for n in range(5))
+                he, me_, ye, de, ae, xe, ce = (
+                    pltpu.roll(value, TILE - 1, 1) for value in (h, mx, my, hd, au, fxx, fxy)
+                )
+                speed = jnp.maximum(au, ae)
+                east_faces = (
+                    (mx + me_) - speed * (he - h),
+                    (fxx + xe) - speed * (me_ - mx),
+                    (fxy + ce) - speed * (ye - my),
+                    de - hd,
+                )
+                x0, x1, x2, x3 = (f - pltpu.roll(f, 1, 1) for f in east_faces)
+                kx = (0.5 * GRAVITY) * (pltpu.roll(g, TILE - 1, 1) - pltpu.roll(g, 1, 1))
+                ups = [U[TPD + side * MOVE + j, q, nxt, :] for q in range(4)]
+                ups += [DA[side, n, nxt, :] for n in (1, 3, 4)]
+                ups.append(arrived_ground[side, 0, j, nxt, :])
+                hn, xn, mn, dn, an, cn, yn, gn = (
+                    jnp.where(sub == 7, pltpu.roll(b, 7, 0), pltpu.roll(a, 7, 0))
+                    for a, b in zip((h, mx, my, hd, av, fxy, fyy, g), ups)
+                )
+                speed = jnp.maximum(av, an)
+                faces = (
+                    (my + mn) - speed * (hn - h),
+                    (fyy + yn) - speed * (mn - my),
+                    (fxy + cn) - speed * (xn - mx),
+                    dn - hd,
+                    gn - g,
+                )
+                rounds = [pltpu.roll(f, 1, 0) for f in faces]
+                lower = [jnp.where(sub == 0, b, a) for a, b in zip(rounds, old)]
+                new_below.extend(rounds)
+                y0, y1, y2, y3 = (n - s for n, s in zip(faces[:4], lower[:4]))
+                ky = (0.5 * GRAVITY) * (faces[4] + lower[4])
+                seep = arrived_ground[side, 1, j, blk, :] * (h + g - hd)
+                R[TPD + side * MOVE + j, 0, blk, :] = -0.5 * (x0 + y0) - seep
+                R[TPD + side * MOVE + j, 1, blk, :] = -0.5 * (x1 + y2) - h * kx
+                R[TPD + side * MOVE + j, 2, blk, :] = -0.5 * (x2 + y1) - h * ky
+                R[TPD + side * MOVE + j, 3, blk, :] = (
+                    arrived_ground[side, 2, j, blk, :] * (x3 + y3) + seep * (1.0 / STORAGE)
+                )
+            return tuple(new_below)
+
+        below = (zero,) * 10
+        for piece, (tile, start, count) in enumerate(PIECES):
+            if tile != j:
+                continue
+            for copy in fields_of(piece):
+                copy.wait_recv()
+            lo, hi = start // 8, (start + count) // 8
+            lax.fori_loop(lo, hi, derive, 0, unroll=4)
+            first = lo - 1 if lo else 0
+            last = hi - 1 if hi < BLOCKS else BLOCKS
+            below = lax.fori_loop(first, last, block, below, unroll=2 if (last - first) % 2 == 0 else 3)
+
+    def fill_lines(tile):
+        side, j = divmod(tile - TPD, MOVE)
+        cols = line_got[side, j, 8:16, :]
+        for q in range(4):
+            for i in range(BLOCKS):
+                blk = rows_of(i)
+                rate = R[tile, q, blk, :]
+                at = q * BLOCKS + i
+                rate = jnp.where(first_lane, pltpu.roll(cols, (TILE - at) % TILE, 1), rate)
+                rate = jnp.where(last_lane, pltpu.roll(cols, TILE // 2 - 1 - at, 1), rate)
+                if i == 0:
+                    rate = jnp.where(sub == 0, line_got[side, j, 4 + q : 5 + q, :], rate)
+                if i == BLOCKS - 1:
+                    rate = jnp.where(sub == 7, line_got[side, j, q : q + 1, :], rate)
+                R[tile, q, blk, :] = rate
 
     def body(step, _):
         send(step)
+
+        @pl.when(step == 0)
+        def _():
+            for load in late:
+                load.wait()
+            ground_slopes()
+            for side in range(2):
+                for j in range(MOVE):
+                    for kind, array in enumerate((G, L, S)):
+                        mover_ground[side, kind, j] = array[leaving[side][j]]
+
+        for copy in grounds(step):
+            copy.start()
         right_sides()
         rims(step)
-        sweep(step + 1, interval(step))
+        sweep(step + 1, interval(step)[1])
         return 0
 
-    lax.fori_loop(0, STEPS, body, 0)
-
-    def movers_of(flags):
-        count = jnp.int32(0)
-        picks = [jnp.int32(0), jnp.int32(0)]
-        for t in range(TPD):
-            at = t + odd * (3 - 2 * t)
-            for j in range(MOVE):
-                picks[j] = jnp.where(jnp.logical_and(flags[t], count == j), at, picks[j])
-            count = count + flags[t].astype(jnp.int32)
-        return picks
-
-    targets_of = [dest_ref[base + t] for t in range(TPD)]
-    rightward = movers_of([d >= base + TPD for d in targets_of])
-    leftward = movers_of([d < base for d in targets_of])
-    keep = pltpu.make_async_copy(U.at[:, 0:4], pool_out.at[0:TPD], out_sem.at[0])
-    keep.start()
-    sent = []
+    lax.fori_loop(0, STEPS - 1, body, 0)
+
+    final = STEPS - 1
+    send(final)
     for j in range(MOVE):
-        for side, picks, target in ((0, rightward, after), (1, leftward, before)):
-            for q in range(4):
-                movers[side, j, q] = U[picks[j], q]
-            copy = pltpu.make_async_remote_copy(
-                movers.at[side, j], pool_out.at[TPD + side * MOVE + j],
-                mv_send.at[side, j], mv_recv.at[side, j],
-                device_id=(target,), device_id_type=MESH)
-            copy.start()
-            sent.append(copy)
+        for q in range(4):
+            for i in range(BLOCKS):
+                blk = rows_of(i)
+                own = [U[p, q, blk, :] for p in range(TPD)]
+                for side in range(2):
+                    value = own[0]
+                    for p in range(1, TPD):
+                        value = jnp.where(leaving[side][j] == p, own[p], value)
+                    movers[side, j, q, blk, :] = value
+        for piece in range(len(PIECES)):
+            if PIECES[piece][0] == j:
+                for copy in fields_of(piece):
+                    copy.start()
+    right_sides()
+    rims(final)
+    outer_lines()
+    for copy in lines():
+        copy.start()
+    for kind in range(3):
+        for copy in grounds(kind):
+            copy.wait_recv()
+    for j in range(MOVE):
+        arrived_sides(j)
+    for copy in lines():
+        copy.wait_recv()
+    for tile in range(TPD, TPD + 2 * MOVE):
+        fill_lines(tile)
+    dt = interval(final)[0]
+    keeps = []
+    for k in range(TPD):
+        tile, tile_wet = wanted[k], wanted_wet[k]
+        dt_k = jnp.where(tile_wet == 1, dt, 0.0)
+        for q in range(4):
+            for i in range(BLOCKS):
+                blk = rows_of(i)
+                made[k, q, blk, :] = U[tile, q, blk, :] + dt_k * R[tile, q, blk, :]
+        keep = pltpu.make_async_copy(made.at[k], tiles_out.at[k], out_sem.at[k])
+        keep.start()
+        keeps.append(keep)
     for step in range(STEPS):
         all_rows(step, mx_send).wait()
         for copy in halos(step):
             copy.wait_send()
-    keep.wait()
-    for copy in sent:
-        copy.wait()
-
-
-def pick_kernel(dest_ref, pool, depth_out, flow_out, head_out, held, in_sem, sem):
-    me = lax.axis_index("tiles")
-    base = me * TPD
-    last = DEVICES - 1
-
-    def odd_of(device):
-        return lax.rem(device // 4, 2)
-
-    wanted = [jnp.int32(0)] * TPD
-    odd = odd_of(me)
-    for t in range(TPD):
-        d = dest_ref[base + t]
-        at = t + odd * (3 - 2 * t)
-        for k in range(TPD):
-            wanted[k] = jnp.where(d == base + k, at, wanted[k])
-    rank = jnp.int32(0)
-    for t in range(TPD):
-        d = dest_ref[jnp.maximum(base - TPD, 0) + t]
-        came = jnp.logical_and(d >= base, me > 0)
-        for k in range(TPD):
-            wanted[k] = jnp.where(jnp.logical_and(came, d == base + k), TPD + rank, wanted[k])
-        rank = rank + came.astype(jnp.int32)
-    rank = jnp.int32(0)
-    for t in range(TPD):
-        d = dest_ref[jnp.minimum(base + TPD, last * TPD) + t]
-        came = jnp.logical_and(d < base + TPD, me < last)
-        for k in range(TPD):
-            wanted[k] = jnp.where(
-                jnp.logical_and(came, d == base + k), TPD + MOVE + rank, wanted[k]
-            )
-        rank = rank + came.astype(jnp.int32)
-    fetches = [pltpu.make_async_copy(pool.at[wanted[k]], held.at[k], in_sem.at[k]) for k in range(TPD)]
+    for kind in range(3):
+        for copy in grounds(kind):
+            copy.wait_send()
+    for piece in range(len(PIECES)):
+        for copy in fields_of(piece):
+            copy.wait_send()
+    for copy in lines():
+        copy.wait_send()
+    for keep in keeps:
+        keep.wait()
+
+
+def split_kernel(tiles, depth_out, flow_out, head_out, held, in_sem, sem):
+    fetches = [
+        pltpu.make_async_copy(tiles.at[k], held.at[k], in_sem.at[k]) for k in range(TPD)
+    ]
     for fetch in fetches:
         fetch.start()
     copies = []
@@ -517,20 +708,22 @@
     smem = pl.BlockSpec(memory_space=pltpu.SMEM)
     vm = lambda *shape: pltpu.VMEM(shape + (TILE,), F32)
     dma = pltpu.SemaphoreType.DMA
-    pool = pl.pallas_call(
+    made = pl.pallas_call(
         flood_kernel,
-        out_shape=jax.ShapeDtypeStruct((TPD + 2 * MOVE, 4, TILE, TILE), F32),
+        out_shape=jax.ShapeDtypeStruct((TPD, 4, TILE, TILE), F32),
         in_specs=[smem] * 3 + [hbm] * 6,
         out_specs=hbm,
         scratch_shapes=[
-            vm(TPD, 4, TILE), vm(TPD, 5, TILE), vm(TPD, 4, TILE),
+            vm(TPD + 2 * MOVE, 4, TILE), vm(TPD, 5, TILE), vm(TPD + 2 * MOVE, 4, TILE),
             vm(TPD, TILE), vm(TPD, TILE), vm(TPD, TILE), vm(TPD, TILE), vm(TPD, TILE),
-            vm(TPD, 2, TILE), vm(STEPS + 1, DEVICES),
-            vm(STEPS + 1, 2, 8), vm(STEPS, 2, 8), vm(STEPS + 1, 2, 24), vm(STEPS, 2, 24),
-            vm(2, MOVE, 4, TILE),
+            vm(TPD, 2, TILE), vm(STEPS, DEVICES),
+            vm(STEPS, 2, 8), vm(STEPS, 2, 8), vm(STEPS, 2, 24), vm(STEPS, 2, 24),
+            vm(2, MOVE, 4, TILE), vm(2, 3, MOVE, TILE), vm(2, 3, MOVE, TILE),
+            vm(2, 5, TILE), vm(2, MOVE, 16), vm(2, MOVE, 16), vm(TPD, 4, TILE),
             dma((6, TPD)), dma((STEPS,)), dma((STEPS,)),
             dma((STEPS, 2)), dma((STEPS, 2)), dma((STEPS, 2)), dma((STEPS, 2)),
-            dma((2, MOVE)), dma((2, MOVE)), dma((1,)),
+            dma((2, 3)), dma((2, 3)), dma((2, 3)), dma((2, 3)), dma((2,)), dma((2,)),
+            dma((TPD,)),
         ],
         compiler_params=pltpu.CompilerParams(
             collective_id=0, has_side_effects=True, vmem_limit_bytes=60 << 20
@@ -538,12 +731,12 @@
     )(tile_wet, neighbours.T, destination, depth, velocity, head, terrain, leakance, diffusivity)
     tile = jax.ShapeDtypeStruct((TPD, TILE, TILE), F32)
     return pl.pallas_call(
-        pick_kernel,
+        split_kernel,
         out_shape=(tile, jax.ShapeDtypeStruct((TPD, 2, TILE, TILE), F32), tile),
-        in_specs=[smem, hbm],
+        in_specs=[hbm],
         out_specs=(hbm,) * 3,
         scratch_shapes=[vm(TPD, 4, TILE), dma((TPD,)), dma((3, TPD))],
-    )(destination, pool)
+    )(made)
 
 
 def solution(mesh):

time: 49.5 us -> 46.6 us (0.941)
  Pallas kernels: 48.6 us -> 45.8 us
    pallas_call x2, Pallas kernels: 48.6 us -> 45.8 us  [the longest x1 43.7 us: shards(): pl.pallas_call(flood_kernel, out_shape=jax.ShapeDtypeStruct((TPD, 4, TILE...]
where the time goes in v3:
time: 46.6 us; the launch traced here: 46.4 us
  Pallas kernels  45.8 us (98%)
  between operations  0.64 us (1%)
    pallas_call x1, Pallas kernels, shards(): pl.pallas_call(flood_kernel, out_shape=jax.ShapeDtypeStruct((TPD, 4, TILE...  43.7 us
    pallas_call x1, Pallas kernels, shards(): pl.pallas_call(split_kernel, out_shape=(tile, jax.ShapeDtypeStruct((TPD,...  2.04 us

profile of v3, /device:TPU:0, one launch (start us, length us, event | category | flops | bytes accessed | tf_op | source)
XLA Modules:
  0.0 46.4 jit_solution(7126912485017732026)
XLA Ops:
  0.6 43.7 %shard_map.112.tiles = f32[4,4,128,128]{3,2,1,0:T(8,128)} custom-call(s32[512]{0:T(512)} %wet_ref.1, s32[4,512]{1,0:T(4,128)} %bitcast.1, s32[512]{0:T(512)} %dest_ref.1, f32[4,128,128]{2,1,0:T(8,128)} %depth_in.1, f32[4,2,128,128]{3,2,1,0:T(8,128)} %vel_in.1, f32[4,128,128]{2,1,0:T(8,128)} %head_in.1, f32[4,128,128]{2,1,0:T(8,128)} %terr_in.1, ...), custom_call_target="tpu_custom_call" | custom-call | tf_op jit(solution)/shard_map/pallas_call | solution.py:711
  44.4 2.0 %shard_map.113 = (f32[4,128,128]{2,1,0:T(8,128)}, f32[4,2,128,128]{3,2,1,0:T(8,128)}, f32[4,128,128]{2,1,0:T(8,128)}) custom-call(f32[4,4,128,128]{3,2,1,0:T(8,128)} %shard_map.112.tiles), custom_call_target="tpu_custom_call" | custom-call | tf_op jit(solution)/shard_map/pallas_call | solution.py:733

commit v4 on v3

--- a/solution.py
+++ b/solution.py
@@ -77,9 +77,9 @@
 def flood_kernel(
     wet_ref, link_ref, dest_ref, depth_in, vel_in, head_in, terr_in, leak_in, diff_in,
     tiles_out,
-    U, D, R, G, L, S, KX, KY, VEL, mbuf, ew_own, ew_got, ns_own, ns_got,
-    movers, mover_ground, arrived_ground, DA, line_own, line_got, made,
-    in_sem, mx_send, mx_recv, ew_send, ew_recv, ns_send, ns_recv, mv_send, mv_recv,
+    U, D, R, G, L, S, KX, KY, VEL, mbuf, mtop, ew_own, ew_got, ns_own, ns_got,
+    movers, mover_ground, arrived_ground, slopes, DA, line_own, line_got, made,
+    in_sem, mx_send, mx_recv, mt_sem, ew_send, ew_recv, ns_send, ns_recv, mv_send, mv_recv,
     mg_send, mg_recv, ln_send, ln_recv, out_sem,
 ):
     me = lax.axis_index("tiles")
@@ -130,6 +130,7 @@
     sub = lax.broadcasted_iota(jnp.int32, (8, TILE), 0)
     first_lane = lane == 0
     last_lane = lane == TILE - 1
+    half_lane = lane // 2
     wall_lane = [jnp.where(linked[p][1] >= 0, -1, TILE - 1) for p in range(TPD - 1)]
     wall_back = [jnp.where(linked[p][0] >= 0, -1, 0) for p in range(TPD)]
     zero = jnp.zeros((8, TILE), F32)
@@ -232,9 +233,31 @@
                 mx_send.at[step], mx_recv.at[step],
                 device_id=(target,), device_id_type=MESH).start()
 
-    def all_rows(step, sem):
-        rest = mbuf.at[step, 1:DEVICES]
+    def all_rows(step, sem, rows=DEVICES):
+        rest = mbuf.at[step, 1:rows]
         return pltpu.make_async_copy(rest, rest, sem.at[step])
+
+    near = [item for item in everyone if item[0] < 8]
+    across = [(offset // 8, target) for offset, target in everyone if offset % 8 == 0]
+
+    def send_near(step):
+        for offset, target in near:
+            pltpu.make_async_remote_copy(
+                mbuf.at[step, 0:1], mbuf.at[step, offset : offset + 1],
+                mx_send.at[step], mx_recv.at[step],
+                device_id=(target,), device_id_type=MESH).start()
+
+    def send_across(step):
+        all_rows(step, mx_recv, 8).wait()
+        mtop[0:1, :] = jnp.max(mbuf[step, 0:8, :], axis=0, keepdims=True)
+        for group, target in across:
+            pltpu.make_async_remote_copy(
+                mtop.at[0:1], mtop.at[group : group + 1], mt_sem.at[0], mt_sem.at[1],
+                device_id=(target,), device_id_type=MESH).start()
+
+    def across_rows(which):
+        rest = mtop.at[1:16]
+        return pltpu.make_async_copy(rest, rest, mt_sem.at[which])
 
     def ground_slopes():
         def block(i, below):
@@ -420,8 +443,13 @@
                     R[p, q, at : at + 1, :] += add
 
     def interval(step):
-        all_rows(step, mx_recv).wait()
-        top = jnp.max(jnp.max(mbuf[step], axis=0, keepdims=True), axis=1, keepdims=True)
+        if isinstance(step, int):
+            across_rows(1).wait()
+            tops = mtop[...]
+        else:
+            all_rows(step, mx_recv).wait()
+            tops = mbuf[step]
+        top = jnp.max(jnp.max(tops, axis=0, keepdims=True), axis=1, keepdims=True)
         dt = COURANT / jnp.broadcast_to(top, (8, TILE))
         return dt, [jnp.where(wet[p] == 1, dt, 0.0) for p in range(TPD)]
 
@@ -472,7 +500,7 @@
             for side, target in ((0, after), (1, before))
         ]
 
-    PIECES = ((0, 0, TILE), (1, 0, TILE // 2), (1, TILE // 2, TILE // 2))
+    PIECES = ((0, 0, TILE), (1, 0, 104), (1, 104, 24))
 
     def fields_of(piece):
         j, start, count = PIECES[piece]
@@ -488,7 +516,7 @@
     def lines():
         return [
             pltpu.make_async_remote_copy(
-                line_own.at[side], line_got.at[side], ln_send.at[side], ln_recv.at[side],
+                line_own.at[pl.ds(side * MOVE, MOVE)], line_got.at[pl.ds(side * MOVE, MOVE)], ln_send.at[side], ln_recv.at[side],
                 device_id=(target,), device_id_type=MESH)
             for side, target in ((0, after), (1, before))
         ]
@@ -499,15 +527,34 @@
                 tile = leaving[side][j]
                 acc = zero
                 for q in range(4):
-                    line_own[side, j, q : q + 1, :] = R[tile, q, TILE - 1 : TILE, :]
-                    line_own[side, j, 4 + q : 5 + q, :] = R[tile, q, 0:1, :]
+                    line_own[side * MOVE + j, q : q + 1, :] = R[tile, q, TILE - 1 : TILE, :]
+                    line_own[side * MOVE + j, 4 + q : 5 + q, :] = R[tile, q, 0:1, :]
                     for i in range(BLOCKS):
-                        value = R[tile, q, rows_of(i), :]
                         at = q * BLOCKS + i
-                        acc = jnp.where(lane == at, pltpu.roll(value, at, 1), acc)
-                        at += TILE // 2
-                        acc = jnp.where(lane == at, pltpu.roll(value, (at + 1) % TILE, 1), acc)
-                line_own[side, j, 8:16, :] = acc
+                        pair = pltpu.roll(R[tile, q, rows_of(i), :], 2 * at + 1, 1)
+                        acc = jnp.where(half_lane == at, pair, acc)
+                line_own[side * MOVE + j, 8:16, :] = acc
+
+    def arrived_slopes():
+        def block(i, below):
+            blk = rows_of(i)
+            nxt = rows_of(jnp.minimum(i + 1, BLOCKS - 1))
+            new_below = []
+            for n in range(2 * MOVE):
+                side, j = divmod(n, MOVE)
+                g = arrived_ground[side, 0, j, blk, :]
+                up = pltpu.roll(arrived_ground[side, 0, j, nxt, :], 7, 0)
+                rise = jnp.where(sub == 7, up, pltpu.roll(g, 7, 0)) - g
+                back = pltpu.roll(rise, 1, 0)
+                new_below.append(back)
+                across_x = pltpu.roll(g, TILE - 1, 1) - pltpu.roll(g, 1, 1)
+                slopes[side, j, 0, blk, :] = (0.5 * GRAVITY) * across_x
+                slopes[side, j, 1, blk, :] = (0.5 * GRAVITY) * (
+                    rise + jnp.where(sub == 0, below[n], back)
+                )
+            return tuple(new_below)
+
+        lax.fori_loop(0, BLOCKS, block, (zero,) * (2 * MOVE), unroll=2)
 
     def arrived_sides(j):
         def derive(i, _):
@@ -531,7 +578,7 @@
             nxt = rows_of(jnp.minimum(i + 1, BLOCKS - 1))
             new_below = []
             for side in range(2):
-                old = below[5 * side : 5 * side + 5]
+                old = below[4 * side : 4 * side + 4]
                 h, mx, my, hd = (U[TPD + side * MOVE + j, q, blk, :] for q in range(4))
                 g = arrived_ground[side, 0, j, blk, :]
                 au, av, fxx, fxy, fyy = (DA[side, n, blk, :] for n in range(5))
@@ -546,13 +593,12 @@
                     de - hd,
                 )
                 x0, x1, x2, x3 = (f - pltpu.roll(f, 1, 1) for f in east_faces)
-                kx = (0.5 * GRAVITY) * (pltpu.roll(g, TILE - 1, 1) - pltpu.roll(g, 1, 1))
+                kx, ky = (slopes[side, j, n, blk, :] for n in range(2))
                 ups = [U[TPD + side * MOVE + j, q, nxt, :] for q in range(4)]
                 ups += [DA[side, n, nxt, :] for n in (1, 3, 4)]
-                ups.append(arrived_ground[side, 0, j, nxt, :])
-                hn, xn, mn, dn, an, cn, yn, gn = (
+                hn, xn, mn, dn, an, cn, yn = (
                     jnp.where(sub == 7, pltpu.roll(b, 7, 0), pltpu.roll(a, 7, 0))
-                    for a, b in zip((h, mx, my, hd, av, fxy, fyy, g), ups)
+                    for a, b in zip((h, mx, my, hd, av, fxy, fyy), ups)
                 )
                 speed = jnp.maximum(av, an)
                 faces = (
@@ -560,13 +606,11 @@
                     (fyy + yn) - speed * (mn - my),
                     (fxy + cn) - speed * (xn - mx),
                     dn - hd,
-                    gn - g,
                 )
                 rounds = [pltpu.roll(f, 1, 0) for f in faces]
                 lower = [jnp.where(sub == 0, b, a) for a, b in zip(rounds, old)]
                 new_below.extend(rounds)
-                y0, y1, y2, y3 = (n - s for n, s in zip(faces[:4], lower[:4]))
-                ky = (0.5 * GRAVITY) * (faces[4] + lower[4])
+                y0, y1, y2, y3 = (n - s for n, s in zip(faces, lower))
                 seep = arrived_ground[side, 1, j, blk, :] * (h + g - hd)
                 R[TPD + side * MOVE + j, 0, blk, :] = -0.5 * (x0 + y0) - seep
                 R[TPD + side * MOVE + j, 1, blk, :] = -0.5 * (x1 + y2) - h * kx
@@ -576,33 +620,20 @@
                 )
             return tuple(new_below)
 
-        below = (zero,) * 10
+        below = (zero,) * 8
         for piece, (tile, start, count) in enumerate(PIECES):
             if tile != j:
                 continue
             for copy in fields_of(piece):
                 copy.wait_recv()
             lo, hi = start // 8, (start + count) // 8
-            lax.fori_loop(lo, hi, derive, 0, unroll=4)
+            whole = hi - (hi - lo) % 4
+            lax.fori_loop(lo, whole, derive, 0, unroll=4)
+            for i in range(whole, hi):
+                derive(i, 0)
             first = lo - 1 if lo else 0
             last = hi - 1 if hi < BLOCKS else BLOCKS
-            below = lax.fori_loop(first, last, block, below, unroll=2 if (last - first) % 2 == 0 else 3)
-
-    def fill_lines(tile):
-        side, j = divmod(tile - TPD, MOVE)
-        cols = line_got[side, j, 8:16, :]
-        for q in range(4):
-            for i in range(BLOCKS):
-                blk = rows_of(i)
-                rate = R[tile, q, blk, :]
-                at = q * BLOCKS + i
-                rate = jnp.where(first_lane, pltpu.roll(cols, (TILE - at) % TILE, 1), rate)
-                rate = jnp.where(last_lane, pltpu.roll(cols, TILE // 2 - 1 - at, 1), rate)
-                if i == 0:
-                    rate = jnp.where(sub == 0, line_got[side, j, 4 + q : 5 + q, :], rate)
-                if i == BLOCKS - 1:
-                    rate = jnp.where(sub == 7, line_got[side, j, q : q + 1, :], rate)
-                R[tile, q, blk, :] = rate
+            below = lax.fori_loop(first, last, block, below, unroll=4)
 
     def body(step, _):
         send(step)
@@ -627,8 +658,11 @@
     lax.fori_loop(0, STEPS - 1, body, 0)
 
     final = STEPS - 1
-    send(final)
-    for j in range(MOVE):
+    for copy in halos(final):
+        copy.start()
+    send_near(final)
+
+    def collect(j):
         for q in range(4):
             for i in range(BLOCKS):
                 blk = rows_of(i)
@@ -638,40 +672,63 @@
                     for p in range(1, TPD):
                         value = jnp.where(leaving[side][j] == p, own[p], value)
                     movers[side, j, q, blk, :] = value
+
+    def send_fields(j):
         for piece in range(len(PIECES)):
             if PIECES[piece][0] == j:
                 for copy in fields_of(piece):
                     copy.start()
+
+    collect(0)
+    send_fields(0)
+    collect(1)
     right_sides()
+    send_across(final)
+    send_fields(1)
+    for kind in range(3):
+        for copy in grounds(kind):
+            copy.wait_recv()
+    arrived_slopes()
     rims(final)
     outer_lines()
     for copy in lines():
         copy.start()
-    for kind in range(3):
-        for copy in grounds(kind):
-            copy.wait_recv()
     for j in range(MOVE):
         arrived_sides(j)
     for copy in lines():
         copy.wait_recv()
-    for tile in range(TPD, TPD + 2 * MOVE):
-        fill_lines(tile)
     dt = interval(final)[0]
     keeps = []
     for k in range(TPD):
-        tile, tile_wet = wanted[k], wanted_wet[k]
-        dt_k = jnp.where(tile_wet == 1, dt, 0.0)
+        tile = wanted[k]
+        dt_k = jnp.where(wanted_wet[k] == 1, dt, 0.0)
+        guest = tile >= TPD
+        line = jnp.maximum(tile - TPD, 0)
+        turned_lane = lax.rem(lane + 1, TILE)
+        edge_lane = turned_lane < jnp.where(guest, 2, 0)
+        south_row = sub == jnp.where(guest, 0, -1)
+        north_row = sub == jnp.where(guest, 7, -1)
+        cols = line_got[line, 8:16, :]
+        rows = line_got[line, 0:8, :]
         for q in range(4):
             for i in range(BLOCKS):
                 blk = rows_of(i)
-                made[k, q, blk, :] = U[tile, q, blk, :] + dt_k * R[tile, q, blk, :]
+                rate = R[tile, q, blk, :]
+                at = q * BLOCKS + i
+                rate = jnp.where(edge_lane, pltpu.roll(cols, TILE - 1 - 2 * at, 1), rate)
+                if i == 0:
+                    rate = jnp.where(south_row, rows[4 + q : 5 + q, :], rate)
+                if i == BLOCKS - 1:
+                    rate = jnp.where(north_row, rows[q : q + 1, :], rate)
+                made[k, q, blk, :] = U[tile, q, blk, :] + dt_k * rate
         keep = pltpu.make_async_copy(made.at[k], tiles_out.at[k], out_sem.at[k])
         keep.start()
         keeps.append(keep)
     for step in range(STEPS):
-        all_rows(step, mx_send).wait()
+        all_rows(step, mx_send, DEVICES if step < final else 8).wait()
         for copy in halos(step):
             copy.wait_send()
+    across_rows(0).wait()
     for kind in range(3):
         for copy in grounds(kind):
             copy.wait_send()
@@ -716,11 +773,11 @@
         scratch_shapes=[
             vm(TPD + 2 * MOVE, 4, TILE), vm(TPD, 5, TILE), vm(TPD + 2 * MOVE, 4, TILE),
             vm(TPD, TILE), vm(TPD, TILE), vm(TPD, TILE), vm(TPD, TILE), vm(TPD, TILE),
-            vm(TPD, 2, TILE), vm(STEPS, DEVICES),
+            vm(TPD, 2, TILE), vm(STEPS, DEVICES), vm(16),
             vm(STEPS, 2, 8), vm(STEPS, 2, 8), vm(STEPS, 2, 24), vm(STEPS, 2, 24),
-            vm(2, MOVE, 4, TILE), vm(2, 3, MOVE, TILE), vm(2, 3, MOVE, TILE),
-            vm(2, 5, TILE), vm(2, MOVE, 16), vm(2, MOVE, 16), vm(TPD, 4, TILE),
-            dma((6, TPD)), dma((STEPS,)), dma((STEPS,)),
+            vm(2, MOVE, 4, TILE), vm(2, 3, MOVE, TILE), vm(2, 3, MOVE, TILE), vm(2, MOVE, 2, TILE),
+            vm(2, 5, TILE), vm(2 * MOVE, 16), vm(2 * MOVE, 16), vm(TPD, 4, TILE),
+            dma((6, TPD)), dma((STEPS,)), dma((STEPS,)), dma((2,)),
             dma((STEPS, 2)), dma((STEPS, 2)), dma((STEPS, 2)), dma((STEPS, 2)),
             dma((2, 3)), dma((2, 3)), dma((2, 3)), dma((2, 3)), dma((2,)), dma((2,)),
             dma((TPD,)),

time: 46.6 us -> 45.2 us (0.970)
  Pallas kernels: 45.8 us -> 44.2 us
    pallas_call x1, Pallas kernels: 43.7 us -> 42.2 us  [shards(): pl.pallas_call(flood_kernel, out_shape=jax.ShapeDtypeStruct((TPD, 4, TILE...]
where the time goes in v4:
time: 45.2 us; the launch traced here: 44.8 us
  Pallas kernels  44.2 us (98%)
  between operations  0.64 us (1%)
    pallas_call x1, Pallas kernels, shards(): pl.pallas_call(flood_kernel, out_shape=jax.ShapeDtypeStruct((TPD, 4, TILE...  42.2 us
    pallas_call x1, Pallas kernels, shards(): pl.pallas_call(split_kernel, out_shape=(tile, jax.ShapeDtypeStruct((TPD,...  2.04 us

profile of v4, /device:TPU:0, one launch (start us, length us, event | category | flops | bytes accessed | tf_op | source)
XLA Modules:
  0.0 44.8 jit_solution(9614694642206071808)
XLA Ops:
  0.6 42.2 %shard_map.112.tiles = f32[4,4,128,128]{3,2,1,0:T(8,128)} custom-call(s32[512]{0:T(512)} %wet_ref.1, s32[4,512]{1,0:T(4,128)} %bitcast.1, s32[512]{0:T(512)} %dest_ref.1, f32[4,128,128]{2,1,0:T(8,128)} %depth_in.1, f32[4,2,128,128]{3,2,1,0:T(8,128)} %vel_in.1, f32[4,128,128]{2,1,0:T(8,128)} %head_in.1, f32[4,128,128]{2,1,0:T(8,128)} %terr_in.1, ...), custom_call_target="tpu_custom_call" | custom-call | tf_op jit(solution)/shard_map/pallas_call | solution.py:768
  42.8 2.0 %shard_map.113 = (f32[4,128,128]{2,1,0:T(8,128)}, f32[4,2,128,128]{3,2,1,0:T(8,128)}, f32[4,128,128]{2,1,0:T(8,128)}) custom-call(f32[4,4,128,128]{3,2,1,0:T(8,128)} %shard_map.112.tiles), custom_call_target="tpu_custom_call" | custom-call | tf_op jit(solution)/shard_map/pallas_call | solution.py:790

commit v5 on v4

--- a/solution.py
+++ b/solution.py
@@ -77,9 +77,9 @@
 def flood_kernel(
     wet_ref, link_ref, dest_ref, depth_in, vel_in, head_in, terr_in, leak_in, diff_in,
     tiles_out,
-    U, D, R, G, L, S, KX, KY, VEL, mbuf, mtop, ew_own, ew_got, ns_own, ns_got,
+    U, D, R, G, L, S, KX, KY, VEL, mbuf, mtop, ew_own, ew_got, ns_own, ns_got, ground_own, ground_got,
     movers, mover_ground, arrived_ground, slopes, DA, line_own, line_got, made,
-    in_sem, mx_send, mx_recv, mt_sem, ew_send, ew_recv, ns_send, ns_recv, mv_send, mv_recv,
+    in_sem, mx_send, mx_recv, mt_sem, ew_send, ew_recv, ns_send, ns_recv, gr_send, gr_recv, mv_send, mv_recv,
     mg_send, mg_recv, ln_send, ln_recv, out_sem,
 ):
     me = lax.axis_index("tiles")
@@ -156,12 +156,10 @@
     ground_e = ground_w = zero
     for i in range(BLOCKS):
         ground_e, ground_w = ground_block(i, (ground_e, ground_w))
-    for s in range(STEPS):
-        for p in range(TPD):
-            ns_own[s, 0, 16 + p : 17 + p, :] = G[p, TILE - 1 : TILE, :]
-            ns_own[s, 1, 16 + p : 17 + p, :] = G[p, 0:1, :]
-        for k in range(2):
-            ns_own[s, k, 20:24, :] = jnp.zeros((4, TILE), F32)
+    ground_own[...] = jnp.zeros((2, 8, TILE), F32)
+    for p in range(TPD):
+        ground_own[0, p : p + 1, :] = G[p, TILE - 1 : TILE, :]
+        ground_own[1, p : p + 1, :] = G[p, 0:1, :]
 
     def sweep(step, dt_of):
         def block(i, carry):
@@ -220,6 +218,16 @@
                 device_id=(north,), device_id_type=MESH),
             pltpu.make_async_remote_copy(
                 ns_own.at[step, 1], ns_got.at[step, 0], ns_send.at[step, 1], ns_recv.at[step, 0],
+                device_id=(south,), device_id_type=MESH),
+        ]
+
+    def ground_halos():
+        return [
+            pltpu.make_async_remote_copy(
+                ground_own.at[0], ground_got.at[1], gr_send.at[0], gr_recv.at[1],
+                device_id=(north,), device_id_type=MESH),
+            pltpu.make_async_remote_copy(
+                ground_own.at[1], ground_got.at[0], gr_send.at[1], gr_recv.at[0],
                 device_id=(south,), device_id_type=MESH),
         ]
 
@@ -395,16 +403,15 @@
         slope = (0.5 * GRAVITY) * h * ((gg - g) if flip_east else (g - gg))
         return sign * mass, sign * push - slope, sign * carry, ghd - hd
 
-    def row_terms(own, got, k, is_north):
+    def row_terms(own, got, own_ground, got_ground, k, is_north):
         rows = lax.broadcasted_iota(jnp.int32, (TPD, TILE), 0)
         link = jnp.full((TPD, TILE), linked[0][k], jnp.int32)
         for p in range(1, TPD):
             link = jnp.where(rows == p, linked[p][k], link)
-        mine = [own[q * 4 : q * 4 + 4, :] for q in range(5)]
+        mine = [own[q * 4 : q * 4 + 4, :] for q in range(4)] + [own_ground]
+        theirs = [got[q * 4 : q * 4 + 4, :] for q in range(4)] + [got_ground]
         signs = (1.0, 1.0, -1.0, 1.0, 1.0)
-        ghost = [
-            jnp.where(link >= 0, got[q * 4 : q * 4 + 4, :], signs[q] * mine[q]) for q in range(5)
-        ]
+        ghost = [jnp.where(link >= 0, theirs[q], signs[q] * mine[q]) for q in range(5)]
         h, a, n, hd, g = mine
         gh, ga, gn, ghd, gg = ghost
         if is_north:
@@ -434,7 +441,10 @@
                         add = add * S[p, blk, :]
                     R[p, q, blk, :] += jnp.where(at_edge, add, 0.0)
         for side, at in ((0, TILE - 1), (1, 0)):
-            terms = row_terms(ns_own.at[step, side], ns_got.at[step, side], 3 - side, side == 0)
+            terms = row_terms(
+                ns_own.at[step, side], ns_got.at[step, side],
+                ground_own[side, 0:TPD, :], ground_got[side, 0:TPD, :], 3 - side, side == 0,
+            )
             for p in range(TPD):
                 for q in range(4):
                     add = terms[q][p : p + 1, :]
@@ -455,6 +465,8 @@
 
     sweep(0, None)
     pl.semaphore_wait(barrier, DEVICES - 1)
+    for copy in ground_halos():
+        copy.start()
 
     def ranked(flags, values):
         count = jnp.int32(0)
@@ -642,7 +654,6 @@
         def _():
             for load in late:
                 load.wait()
-            ground_slopes()
             for side in range(2):
                 for j in range(MOVE):
                     for kind, array in enumerate((G, L, S)):
@@ -650,7 +661,18 @@
 
         for copy in grounds(step):
             copy.start()
+
+        @pl.when(step == 0)
+        def _():
+            ground_slopes()
+
         right_sides()
+
+        @pl.when(step == 0)
+        def _():
+            for copy in ground_halos():
+                copy.wait_recv()
+
         rims(step)
         sweep(step + 1, interval(step)[1])
         return 0
@@ -658,9 +680,9 @@
     lax.fori_loop(0, STEPS - 1, body, 0)
 
     final = STEPS - 1
+    send_near(final)
     for copy in halos(final):
         copy.start()
-    send_near(final)
 
     def collect(j):
         for q in range(4):
@@ -729,6 +751,8 @@
         for copy in halos(step):
             copy.wait_send()
     across_rows(0).wait()
+    for copy in ground_halos():
+        copy.wait_send()
     for kind in range(3):
         for copy in grounds(kind):
             copy.wait_send()
@@ -774,11 +798,11 @@
             vm(TPD + 2 * MOVE, 4, TILE), vm(TPD, 5, TILE), vm(TPD + 2 * MOVE, 4, TILE),
             vm(TPD, TILE), vm(TPD, TILE), vm(TPD, TILE), vm(TPD, TILE), vm(TPD, TILE),
             vm(TPD, 2, TILE), vm(STEPS, DEVICES), vm(16),
-            vm(STEPS, 2, 8), vm(STEPS, 2, 8), vm(STEPS, 2, 24), vm(STEPS, 2, 24),
+            vm(STEPS, 2, 8), vm(STEPS, 2, 8), vm(STEPS, 2, 16), vm(STEPS, 2, 16), vm(2, 8), vm(2, 8),
             vm(2, MOVE, 4, TILE), vm(2, 3, MOVE, TILE), vm(2, 3, MOVE, TILE), vm(2, MOVE, 2, TILE),
             vm(2, 5, TILE), vm(2 * MOVE, 16), vm(2 * MOVE, 16), vm(TPD, 4, TILE),
             dma((6, TPD)), dma((STEPS,)), dma((STEPS,)), dma((2,)),
-            dma((STEPS, 2)), dma((STEPS, 2)), dma((STEPS, 2)), dma((STEPS, 2)),
+            dma((STEPS, 2)), dma((STEPS, 2)), dma((STEPS, 2)), dma((STEPS, 2)), dma((2,)), dma((2,)),
             dma((2, 3)), dma((2, 3)), dma((2, 3)), dma((2, 3)), dma((2,)), dma((2,)),
             dma((TPD,)),
         ],

time: 45.2 us -> 44.7 us (0.989)
  no operation moved by 1% of the time
where the time goes in v5:
time: 44.7 us; the launch traced here: 44.5 us
  Pallas kernels  43.9 us (98%)
  between operations  0.64 us (1%)
    pallas_call x1, Pallas kernels, shards(): pl.pallas_call(flood_kernel, out_shape=jax.ShapeDtypeStruct((TPD, 4, TILE...  41.8 us
    pallas_call x1, Pallas kernels, shards(): pl.pallas_call(split_kernel, out_shape=(tile, jax.ShapeDtypeStruct((TPD,...  2.04 us

profile of v5, /device:TPU:0, one launch (start us, length us, event | category | flops | bytes accessed | tf_op | source)
XLA Modules:
  0.0 44.5 jit_solution(5804583478352599385)
XLA Ops:
  0.6 41.8 %shard_map.112.tiles = f32[4,4,128,128]{3,2,1,0:T(8,128)} custom-call(s32[512]{0:T(512)} %wet_ref.1, s32[4,512]{1,0:T(4,128)} %bitcast.1, s32[512]{0:T(512)} %dest_ref.1, f32[4,128,128]{2,1,0:T(8,128)} %depth_in.1, f32[4,2,128,128]{3,2,1,0:T(8,128)} %vel_in.1, f32[4,128,128]{2,1,0:T(8,128)} %head_in.1, f32[4,128,128]{2,1,0:T(8,128)} %terr_in.1, ...), custom_call_target="tpu_custom_call" | custom-call | tf_op jit(solution)/shard_map/pallas_call | solution.py:792
  42.5 2.0 %shard_map.113 = (f32[4,128,128]{2,1,0:T(8,128)}, f32[4,2,128,128]{3,2,1,0:T(8,128)}, f32[4,128,128]{2,1,0:T(8,128)}) custom-call(f32[4,4,128,128]{3,2,1,0:T(8,128)} %shard_map.112.tiles), custom_call_target="tpu_custom_call" | custom-call | tf_op jit(solution)/shard_map/pallas_call | solution.py:814

commit v6 on v5

--- a/solution.py
+++ b/solution.py
@@ -387,7 +387,7 @@
                 R[p, 3, blk, :] = S[p, blk, :] * (x3 + y3) + seep * (1.0 / STORAGE)
             return tuple(new_below)
 
-        lax.fori_loop(0, BLOCKS, block, (zero,) * (4 * TPD), unroll=2)
+        lax.fori_loop(0, BLOCKS, block, (zero,) * (4 * TPD), unroll=4)
 
     def column_terms(own, got, link, flip_east):
         ghost = jnp.where(link >= 0, got, jnp.where(lane // BLOCKS == 1, -own, own))

time: 44.7 us -> 44.9 us (level)
  no operation moved by 1% of the time
where the time goes in v6:
time: 44.9 us; the launch traced here: 44.7 us
  Pallas kernels  44 us (98%)
  between operations  0.64 us (1%)
    pallas_call x1, Pallas kernels, shards(): pl.pallas_call(flood_kernel, out_shape=jax.ShapeDtypeStruct((TPD, 4, TILE...  42 us
    pallas_call x1, Pallas kernels, shards(): pl.pallas_call(split_kernel, out_shape=(tile, jax.ShapeDtypeStruct((TPD,...  2.04 us

profile of v6, /device:TPU:0, one launch (start us, length us, event | category | flops | bytes accessed | tf_op | source)
XLA Modules:
  0.0 44.7 jit_solution(16268156051831652199)
XLA Ops:
  0.6 42.0 %shard_map.112.tiles = f32[4,4,128,128]{3,2,1,0:T(8,128)} custom-call(s32[512]{0:T(512)} %wet_ref.1, s32[4,512]{1,0:T(4,128)} %bitcast.1, s32[512]{0:T(512)} %dest_ref.1, f32[4,128,128]{2,1,0:T(8,128)} %depth_in.1, f32[4,2,128,128]{3,2,1,0:T(8,128)} %vel_in.1, f32[4,128,128]{2,1,0:T(8,128)} %head_in.1, f32[4,128,128]{2,1,0:T(8,128)} %terr_in.1, ...), custom_call_target="tpu_custom_call" | custom-call | tf_op jit(solution)/shard_map/pallas_call | solution.py:792
  42.6 2.0 %shard_map.113 = (f32[4,128,128]{2,1,0:T(8,128)}, f32[4,2,128,128]{3,2,1,0:T(8,128)}, f32[4,128,128]{2,1,0:T(8,128)}) custom-call(f32[4,4,128,128]{3,2,1,0:T(8,128)} %shard_map.112.tiles), custom_call_target="tpu_custom_call" | custom-call | tf_op jit(solution)/shard_map/pallas_call | solution.py:814
